TPU v7x, 256 devices: a whole 4x4x8 slice. The times are simulated.
256 devices in a mesh: band: 128 (over z, y, x), feat: 2 (over core).
Axes of the slice: x: 4, y: 4, z: 8, core: 2. Of those that a mesh axis runs over, the one named last changes fastest.
Arguments:
- grid_latent: bfloat16 [131072, 512], P('band', 'feat'), may hold values from -6 to 6
- mesh_latent: bfloat16 [65536, 512], P('band', 'feat'), may hold values from -6 to 6
- encode_weights: bfloat16 [4, 512, 512], P(None, None, 'feat'), may hold values from -0.25 to 0.25
- layer_weights: bfloat16 [2, 4, 512, 512], P(None, None, None, 'feat'), may hold values from -0.25 to 0.25
- decode_weights: bfloat16 [4, 512, 512], P(None, None, 'feat'), may hold values from -0.25 to 0.25
- encode_senders: int32 [128, 5, 512], P('band'), may hold values from 0 to 1023
- encode_targets: int32 [128, 5, 512], P('band'), may hold values from 0 to 511
- encode_live: int32 [128, 5, 512], P('band'), may hold values from 0 to 1, as said below
- mesh_senders: int32 [65536, 8], P('band'), may hold values from 0 to 65535, as said below
- mesh_live: int32 [65536, 8], P('band'), may hold values 0 or 1
- decode_senders: int32 [128, 5, 1024], P('band'), may hold values from 0 to 511
- decode_targets: int32 [128, 5, 1024], P('band'), may hold values from 0 to 1023
- decode_live: int32 [128, 5, 1024], P('band'), may hold values from 0 to 1, as said below
Outputs:
- mesh_out: bfloat16 [65536, 512], P('band', 'feat')
- grid_out: bfloat16 [131072, 512], P('band', 'feat')
Inputs may be any that keep to these rules, and one draw needn't show every extreme that they name: `encode_live`: A slot is live only where its band d - o + 2 exists; all slots of offset 2 (an owner's own band) are live. `decode_live`: A slot is live only where its owner d - o + 2 exists; all slots of offset 2 (a band's own owner) are live. `mesh_senders`: A mesh node's senders are nodes of its own owner or among the 64 rows at the near end of the owner before or after it.
All inputs are finite; a program needn't handle non-finite values. No bound on the sum of `mesh_live` on one device may be relied on, other than what follows from the above.
Results may differ from a plain program's by a relative error of at most 0.018.
Values may be sent and summed in bfloat16 or wider, within the bound.
No kernel may reach another device: no remote copies, remote signals or barrier semaphores. Data moves between devices by JAX's collectives and lax.ppermute only.
A program may use at most 64 MiB of HBM per device.

v0:
```python
import math

import jax
import jax.numpy as jnp
from jax import lax
from jax.sharding import PartitionSpec as P

REACH = 2
LAYERS = 2


def from_behind(value, axis, steps):
    count = lax.axis_size(axis)
    initial, last = (max(0, -steps), min(count, count - steps))
    return lax.ppermute(value, axis, [(source, source + steps) for source in range(initial, last)])


def with_halo(cells, sides, width):
    for axis, dim in sides:
        count = lax.axis_size(axis)
        ends = count - 1
        head = lax.slice_in_dim(cells, 0, width, axis=dim)
        tail = lax.slice_in_dim(cells, cells.shape[dim] - width, cells.shape[dim], axis=dim)
        cells = jnp.concatenate(
            [
                lax.ppermute(tail, axis, [(i, (i + 1) % count) for i in range(ends)]),
                cells,
                lax.ppermute(head, axis, [((i + 1) % count, i) for i in range(ends)]),
            ],
            axis=dim,
        )
    return cells


def project(latent, weights):
    return jnp.dot(latent, weights, preferred_element_type=jnp.float32)


def full_latent(latent):
    return lax.all_gather(latent, "feat", axis=1, tiled=True)


def refresh(latent, latent_full, summed, weights):
    summed_full = lax.all_gather(summed.astype(jnp.bfloat16), "feat", axis=1, tiled=True)
    update = project(latent_full, weights[2]) + project(summed_full, weights[3])
    return (latent.astype(jnp.float32) + jax.nn.silu(update)).astype(jnp.bfloat16)


def aggregate(arrived, targets, live, receiver_side):
    node_count = receiver_side.shape[0]
    col_width = arrived.shape[-1]
    arrived_flat = arrived.reshape(-1, col_width)
    target_flat = targets.reshape(-1)
    live_flat = live.reshape(-1)
    block_rows = math.gcd(arrived_flat.shape[0], 512)
    block_count = arrived_flat.shape[0] // block_rows
    node_ids = jnp.arange(node_count, dtype=jnp.int32)[None, :]

    def one_block(running, block_idx):
        picked = lax.dynamic_slice_in_dim(arrived_flat, block_idx * block_rows, block_rows, 0)
        targets_block = lax.dynamic_slice_in_dim(target_flat, block_idx * block_rows, block_rows, 0)
        flags_block = lax.dynamic_slice_in_dim(live_flat, block_idx * block_rows, block_rows, 0)
        preact = picked.astype(jnp.float32) + receiver_side[targets_block]
        message = (jax.nn.silu(preact) * flags_block[:, None].astype(jnp.float32)).astype(
            jnp.bfloat16
        )
        one_hot = (targets_block[:, None] == node_ids).astype(jnp.bfloat16)
        running = running + lax.dot_general(
            one_hot, message, (((0,), (0,)), ((), ())), preferred_element_type=jnp.float32
        )
        return (running, None)

    summed, _ = lax.scan(
        one_block,
        jnp.zeros((node_count, col_width), jnp.float32),
        jnp.arange(block_count, dtype=jnp.int32),
    )
    return summed


def owner_pieces(outgoing):
    pieces = []
    for offset in range(2 * REACH + 1):
        if offset == REACH:
            pieces.append(outgoing[offset])
        else:
            pieces.append(from_behind(outgoing[offset], "band", offset - REACH))
    return jnp.stack(pieces, axis=0)


def band_pieces(decode_sent, senders):
    pieces = []
    for offset in range(2 * REACH + 1):
        if offset == REACH:
            source_rows = decode_sent
        else:
            source_rows = from_behind(decode_sent, "band", offset - REACH)
        pieces.append(source_rows[senders[offset]])
    return jnp.stack(pieces, axis=0)


def mesh_messages(extended, receiver_side, local_senders, live):
    preact = extended[local_senders].astype(jnp.float32) + receiver_side[:, None, :]
    message = (jax.nn.silu(preact) * live[..., None].astype(jnp.float32)).astype(jnp.bfloat16)
    return jnp.sum(message.astype(jnp.float32), axis=1)


def body(
    grid_latent,
    mesh_latent,
    encode_weights,
    layer_weights,
    decode_weights,
    encode_senders,
    encode_targets,
    encode_live,
    mesh_senders,
    mesh_live,
    decode_senders,
    decode_targets,
    decode_live,
):
    mesh_rows = mesh_latent.shape[0]
    margin = mesh_rows // 8
    grid_full = full_latent(grid_latent)
    mesh_full = full_latent(mesh_latent)
    encode_sent = project(grid_full, encode_weights[0]).astype(jnp.bfloat16)
    outgoing = encode_sent[encode_senders[0]]
    arrived = owner_pieces(outgoing)
    encode_recv = project(mesh_full, encode_weights[1])
    encode_sum = aggregate(arrived, encode_targets[0], encode_live[0], encode_recv)
    mesh_now = refresh(mesh_latent, mesh_full, encode_sum, encode_weights)
    local_senders = mesh_senders - (lax.axis_index("band") * mesh_rows - margin)
    for layer_idx in range(LAYERS):
        weights = layer_weights[layer_idx]
        layer_full = full_latent(mesh_now)
        layer_sent = project(layer_full, weights[0]).astype(jnp.bfloat16)
        extended = with_halo(layer_sent, (("band", 0),), margin)
        layer_recv = project(layer_full, weights[1])
        summed = mesh_messages(extended, layer_recv, local_senders, mesh_live)
        mesh_now = refresh(mesh_now, layer_full, summed, weights)
    mesh_full = full_latent(mesh_now)
    decode_sent = project(mesh_full, decode_weights[0]).astype(jnp.bfloat16)
    arrived = band_pieces(decode_sent, decode_senders[0])
    decode_recv = project(grid_full, decode_weights[1])
    decode_sum = aggregate(arrived, decode_targets[0], decode_live[0], decode_recv)
    grid_now = refresh(grid_latent, grid_full, decode_sum, decode_weights)
    return (mesh_now, grid_now)


def solution(mesh):
    placed = (
        P("band", "feat"),
        P("band", "feat"),
        P(None, None, "feat"),
        P(None, None, None, "feat"),
        P(None, None, "feat"),
        P("band", None, None),
        P("band", None, None),
        P("band", None, None),
        P("band", None),
        P("band", None),
        P("band", None, None),
        P("band", None, None),
        P("band", None, None),
    )
    return jax.shard_map(
        body,
        mesh=mesh,
        in_specs=placed,
        out_specs=(P("band", "feat"), P("band", "feat")),
        check_vma=False,
    )
```

profile of v0, /device:TPU:129, one launch (start us, length us, event | category | flops | bytes accessed | tf_op | source)
XLA Modules:
  0.0 316.8 jit_solution(3605887837495028650)
XLA Ops:
  13.9 12.3 %all-gather.3.cloned.1.call-done = bf16[1024,512]{1,0:T(8,128)(2,1)} async-done(((bf16[1024,256]{1,0:T(8,128)(2,1)}), bf16[1024,512]{1,0:T(8,128)(2,1)}) %all-gather.3.cloned.1.call-update) | async-done | bytes 1048592 | tf_op jit(solution)/shard_map/all_gather | solution.py:40
  27.8 7.6 %gather_fusion.2 = bf16[2560,256]{1,0:T(8,128)(2,1)S(1)} fusion(bf16[1024,256]{1,0:T(8,128)(2,1)S(1)} %convolution_convert_fusion, s32[3072]{0:T(1024)S(1)} %pad_clamp_fusion.2), kind=kCustom, calls=%fused_computation.2 | custom fusion | bytes 2631680 | tf_op jit(solution)/shard_map/gather | solution.py:128
  36.4 6.7 %collective-permute-start = (bf16[512,256]{1,0:T(8,128)(2,1)}, bf16[512,256]{1,0:T(8,128)(2,1)S(1)}, u32[]{:S(2)}, u32[]{:S(2)}) collective-permute-start(bf16[512,256]{1,0:T(8,128)(2,1)} %get-tuple-element.177), channel_id=1, source_target_pairs={{4,0},{6,2},{8,4},{10,6},{12,8},{14,10},{16,12},{18,14},{20,16},{2... | collective-permute-start | bytes 786440 | tf_op jit(solution)/shard_map/ppermute | solution.py:15
  51.3 5.8 %collective-permute-done.1 = bf16[512,256]{1,0:T(8,128)(2,1)} collective-permute-done((bf16[512,256]{1,0:T(8,128)(2,1)}, bf16[512,256]{1,0:T(8,128)(2,1)}, u32[]{:S(2)}, u32[]{:S(2)}) %collective-permute-start.1) | collective-permute-done | bytes 262176 | tf_op jit(solution)/shard_map/ppermute | solution.py:15
  58.1 3.8 %collective-permute-done.2 = bf16[512,256]{1,0:T(8,128)(2,1)S(1)} collective-permute-done((bf16[512,256]{1,0:T(8,128)(2,1)}, bf16[512,256]{1,0:T(8,128)(2,1)S(1)}, u32[]{:S(2)}, u32[]{:S(2)}) %collective-permute-start.2) | collective-permute-done | bytes 262176 | tf_op jit(solution)/shard_map/ppermute | solution.py:15
  61.9 3.9 %collective-permute-done.3 = bf16[512,256]{1,0:T(8,128)(2,1)S(1)} collective-permute-done((bf16[512,256]{1,0:T(8,128)(2,1)}, bf16[512,256]{1,0:T(8,128)(2,1)S(1)}, u32[]{:S(2)}, u32[]{:S(2)}) %collective-permute-start.3) | collective-permute-done | bytes 262176 | tf_op jit(solution)/shard_map/ppermute | solution.py:15
  66.9 23.2 %while.22 = (s32[]{:T(128)}, f32[512,256]{1,0:T(8,128)S(1)}, s32[5]{0:T(128)S(1)}, s32[2560]{0:T(1024)S(1)}, bf16[2560,256]{1,0:T(8,128)(2,1)}, /*index=5*/f32[5...) while((s32[]{:T(128)}, f32[512,256]{1,0:T(8,128)S(1)}, ...), condition=%wide.region_1.2_spmd.clone, body=%wide.region_0.1_spmd.clone.sunk | while | flops 135793664 | bytes 2906297 | solution.py:73
  90.2 4.1 %all_gather.29 = bf16[512,512]{1,0:T(8,128)(2,1)S(1)} all-gather(bf16[512,256]{1,0:T(8,128)(2,1)S(1)} %convert_element_type.87), channel_id=1, replica_groups=mesh['band'=128,'feat'=2] {'feat'}, dimensions={1}, use_global_device_ids=true | all-gather | bytes 786432 | tf_op jit(solution)/shard_map/all_gather | solution.py:44
  102.8 8.2 %collective-permute-start.5 = (bf16[64,256]{1,0:T(8,128)(2,1)S(1)}, bf16[64,256]{1,0:T(8,128)(2,1)S(1)}, u32[]{:S(2)}, u32[]{:S(2)}) collective-permute-start(bf16[64,256]{1,0:T(8,128)(2,1)S(1)} %get-tuple-element.181), channel_id=1, source_target_pairs={{2,0},{4,2},{6,4},{8,6},{10,8},{12,10},{14,12},{16,14},{18,16},{20... | collective-permute-start | bytes 98312 | tf_op jit(solution)/shard_map/ppermute | solution.py:28
  113.1 14.6 %gather_fusion.3 = bf16[4096,256]{1,0:T(8,128)(2,1)S(1)} fusion(bf16[640,256]{1,0:T(8,128)(2,1)S(1)} %pad_maximum_fusion, s32[4096]{0:T(1024)S(1)} %broadcast_clamp_fusion), kind=kCustom, calls=%fused_computation.3 | custom fusion | bytes 4210688 | tf_op jit(solution)/shard_map/gather | solution.py:103
  138.5 8.9 %collective-permute-start.7 = (bf16[64,256]{1,0:T(8,128)(2,1)S(1)}, bf16[64,256]{1,0:T(8,128)(2,1)S(1)}, u32[]{:S(2)}, u32[]{:S(2)}) collective-permute-start(bf16[64,256]{1,0:T(8,128)(2,1)S(1)} %get-tuple-element.179), channel_id=1, source_target_pairs={{2,0},{4,2},{6,4},{8,6},{10,8},{12,10},{14,12},{16,14},{18,16},{20... | collective-permute-start | bytes 98312 | tf_op jit(solution)/shard_map/ppermute | solution.py:28
  148.5 14.6 %gather_fusion.4 = bf16[4096,256]{1,0:T(8,128)(2,1)S(1)} fusion(bf16[640,256]{1,0:T(8,128)(2,1)S(1)} %pad_maximum_fusion.1, s32[4096]{0:T(1024)S(1)} %broadcast_clamp_fusion), kind=kCustom, calls=%fused_computation.4 | custom fusion | bytes 4210688 | tf_op jit(solution)/shard_map/gather | solution.py:103
  173.1 5.2 %collective-permute-start.8 = (bf16[512,256]{1,0:T(8,128)(2,1)S(1)}, bf16[512,256]{1,0:T(8,128)(2,1)S(1)}, u32[]{:S(2)}, u32[]{:S(2)}) collective-permute-start(bf16[512,256]{1,0:T(8,128)(2,1)S(1)} %convolution_convert_fusion.1), channel_id=1, source_target_pairs={{4,0},{6,2},{8,4},{10,6},{12,8},{14,10},{16,12},{18,14},{20,16},{2... | collective-permute-start | bytes 786440 | tf_op jit(solution)/shard_map/ppermute | solution.py:15
  178.3 6.3 %collective-permute-start.9 = (bf16[512,256]{1,0:T(8,128)(2,1)S(1)}, bf16[512,256]{1,0:T(8,128)(2,1)S(1)}, u32[]{:S(2)}, u32[]{:S(2)}) collective-permute-start(bf16[512,256]{1,0:T(8,128)(2,1)S(1)} %convolution_convert_fusion.1), channel_id=1, source_target_pairs={{2,0},{4,2},{6,4},{8,6},{10,8},{12,10},{14,12},{16,14},{18,16},{20... | collective-permute-start | bytes 786440 | tf_op jit(solution)/shard_map/ppermute | solution.py:15
  187.5 3.7 %collective-permute-start.11 = (bf16[512,256]{1,0:T(8,128)(2,1)S(1)}, bf16[512,256]{1,0:T(8,128)(2,1)S(1)}, u32[]{:S(2)}, u32[]{:S(2)}) collective-permute-start(bf16[512,256]{1,0:T(8,128)(2,1)S(1)} %convolution_convert_fusion.1), channel_id=1, source_target_pairs={{0,4},{2,6},{4,8},{6,10},{8,12},{10,14},{12,16},{14,18},{16,20},{1... | collective-permute-start | bytes 786440 | tf_op jit(solution)/shard_map/ppermute | solution.py:15
  191.2 4.9 %gather_fusion.7 = bf16[1024,256]{1,0:T(8,128)(2,1)} fusion(bf16[512,256]{1,0:T(8,128)(2,1)S(1)} %convolution_convert_fusion.1, s32[1024]{0:T(1024)S(1)} %get-tuple-element.187), kind=kCustom, calls=%fused_computation.7 | custom fusion | bytes 1052672 | tf_op jit(solution)/shard_map/gather | solution.py:98
  196.2 5.0 %gather_fusion.5 = bf16[1024,256]{1,0:T(8,128)(2,1)} fusion(bf16[512,256]{1,0:T(8,128)(2,1)S(1)} %collective-permute-done.8, s32[1024]{0:T(1024)S(1)} %broadcast_clamp_fusion.5), kind=kCustom, calls=%fused_computation.5 | custom fusion | bytes 1052672 | tf_op jit(solution)/shard_map/gather | solution.py:98
  203.0 5.0 %gather_fusion.6 = bf16[1024,256]{1,0:T(8,128)(2,1)} fusion(bf16[512,256]{1,0:T(8,128)(2,1)S(1)} %collective-permute-done.9, s32[1024]{0:T(1024)S(1)} %get-tuple-element.188), kind=kCustom, calls=%fused_computation.6 | custom fusion | bytes 1052672 | tf_op jit(solution)/shard_map/gather | solution.py:98
  211.8 3.9 %gather_fusion.8 = bf16[1024,256]{1,0:T(8,128)(2,1)S(1)} fusion(bf16[512,256]{1,0:T(8,128)(2,1)S(1)} %collective-permute-done.10, s32[1024]{0:T(1024)S(1)} %broadcast_clamp_fusion.2), kind=kCustom, calls=%fused_computation.8 | custom fusion | bytes 1052672 | tf_op jit(solution)/shard_map/gather | solution.py:98
  216.6 3.9 %gather_fusion.9 = bf16[1024,256]{1,0:T(8,128)(2,1)S(1)} fusion(bf16[512,256]{1,0:T(8,128)(2,1)S(1)} %collective-permute-done.11, s32[1024]{0:T(1024)S(1)} %broadcast_clamp_fusion.1), kind=kCustom, calls=%fused_computation.9 | custom fusion | bytes 1052672 | tf_op jit(solution)/shard_map/gather | solution.py:98
  221.3 67.9 %while.23 = (s32[]{:T(128)}, f32[1024,256]{1,0:T(8,128)}, s32[10]{0:T(128)S(1)}, s32[5120]{0:T(1024)}, bf16[5120,256]{1,0:T(8,128)(2,1)}, /*index=5*/f32[1024,25...) while((s32[]{:T(128)}, f32[1024,256]{1,0:T(8,128)}, ...), condition=%wide.region_5.6_spmd.clone, body=%wide.region_4.5_spmd.clone.sunk | while | flops 270535680 | bytes 3954873 | solution.py:73
  231.4 3.2 %fusion.96 = f32[1024,256]{1,0:T(8,128)} fusion(f32[1024,256]{1,0:T(8,128)} %get-tuple-element.332, s32[512]{0:T(512)S(1)} %get-tuple-element.284, pred[]{:T(512)S(6)} %compare.7, f32[512,256]{1,0:T(8,128)S(1)} %gather_fusion.1, f32[512]{0:T(512)S(1)} %get-tuple-element.286, bf16[5120,256]{1,0:T(8,128)(2,1)} %get-tuple-element.346, s32[]{:T(128)S(6)} %select_n.109), kind=kOutput, calls=%fused_computation.26.clone.1 | convolution fusion | flops 270532608 | bytes 2887685 | tf_op jit(solution)/shard_map/while/body/eval_jaxpr/dot_general | solution.py:68
  238.2 3.2 %fusion.96 = f32[1024,256]{1,0:T(8,128)} fusion(f32[1024,256]{1,0:T(8,128)} %get-tuple-element.332, s32[512]{0:T(512)S(1)} %get-tuple-element.284, pred[]{:T(512)S(6)} %compare.7, f32[512,256]{1,0:T(8,128)S(1)} %gather_fusion.1, f32[512]{0:T(512)S(1)} %get-tuple-element.286, bf16[5120,256]{1,0:T(8,128)(2,1)} %get-tuple-element.346, s32[]{:T(128)S(6)} %select_n.109), kind=kOutput, calls=%fused_computation.26.clone.1 | convolution fusion | flops 270532608 | bytes 2887685 | tf_op jit(solution)/shard_map/while/body/eval_jaxpr/dot_general | solution.py:68
  292.7 14.7 %all-gather.5.cloned.1.call-done = bf16[1024,512]{1,0:T(8,128)(2,1)} async-done(((bf16[1024,256]{1,0:T(8,128)(2,1)}), bf16[1024,512]{1,0:T(8,128)(2,1)}) %all-gather.5.cloned.1.call-update) | async-done | bytes 1048592 | tf_op jit(solution)/shard_map/all_gather | solution.py:44
  (185 shorter events, 142.5 us)
Async XLA Ops:
  7.2 6.1 %copy-start.5 = (bf16[4,512,256]{2,1,0:T(8,128)(2,1)S(1)}, bf16[4,512,256]{2,1,0:T(8,128)(2,1)}, u32[]{:S(2)}) copy-start(bf16[4,512,256]{2,1,0:T(8,128)(2,1)} %param.19) | copy-start | bytes 3145732
  7.2 19.0 %all-gather.3.cloned.1.call-start = ((), (), s32[]{:S(2)}) async-start(), calls=%async_computation | async-start | bytes 1572864 | tf_op jit(solution)/shard_map/all_gather | solution.py:40
  7.9 299.5 %all-gather.5.cloned.1.call-start = ((), (), s32[]{:S(2)}) async-start(), calls=%async_computation.1 | async-start | bytes 1572864 | tf_op jit(solution)/shard_map/all_gather | solution.py:44
  35.4 10.5 %copy-start.13 = (s32[1,5,512]{2,0,1:T(1,128)S(1)}, s32[1,5,512]{2,0,1:T(1,128)}, u32[]{:S(2)}) copy-start(s32[1,5,512]{2,0,1:T(1,128)} %param.23) | copy-start | bytes 30724
  35.4 10.6 %copy-start.14 = (s32[1,5,512]{2,0,1:T(1,128)S(1)}, s32[1,5,512]{2,0,1:T(1,128)}, u32[]{:S(2)}) copy-start(s32[1,5,512]{2,0,1:T(1,128)} %param.24) | copy-start | bytes 30724
  35.4 10.6 %copy-start.12 = (s32[512,8]{0,1:T(8,128)S(1)}, s32[512,8]{0,1:T(8,128)}, u32[]{:S(2)}) copy-start(s32[512,8]{0,1:T(8,128)} %param.26) | copy-start | bytes 49156
  36.4 14.8 %collective-permute-start = (bf16[512,256]{1,0:T(8,128)(2,1)}, bf16[512,256]{1,0:T(8,128)(2,1)S(1)}, u32[]{:S(2)}, u32[]{:S(2)}) collective-permute-start(bf16[512,256]{1,0:T(8,128)(2,1)} %get-tuple-element.177), channel_id=1, source_target_pairs={{4,0},{6,2},{8,4},{10,6},{12,8},{14,10},{16,12},{18,14},{20,16},{2... | collective-permute-start | bytes 786440 | tf_op jit(solution)/shard_map/ppermute | solution.py:15
  43.1 13.9 %collective-permute-start.1 = (bf16[512,256]{1,0:T(8,128)(2,1)}, bf16[512,256]{1,0:T(8,128)(2,1)}, u32[]{:S(2)}, u32[]{:S(2)}) collective-permute-start(bf16[512,256]{1,0:T(8,128)(2,1)} %get-tuple-element.176), channel_id=1, source_target_pairs={{2,0},{4,2},{6,4},{8,6},{10,8},{12,10},{14,12},{16,14},{18,16},{20... | collective-permute-start | bytes 786440 | tf_op jit(solution)/shard_map/ppermute | solution.py:15
  46.2 15.6 %collective-permute-start.2 = (bf16[512,256]{1,0:T(8,128)(2,1)}, bf16[512,256]{1,0:T(8,128)(2,1)S(1)}, u32[]{:S(2)}, u32[]{:S(2)}) collective-permute-start(bf16[512,256]{1,0:T(8,128)(2,1)} %get-tuple-element.175), channel_id=1, source_target_pairs={{0,2},{2,4},{4,6},{6,8},{8,10},{10,12},{12,14},{14,16},{16,18},{18... | collective-permute-start | bytes 786440 | tf_op jit(solution)/shard_map/ppermute | solution.py:15
  48.7 17.1 %collective-permute-start.3 = (bf16[512,256]{1,0:T(8,128)(2,1)}, bf16[512,256]{1,0:T(8,128)(2,1)S(1)}, u32[]{:S(2)}, u32[]{:S(2)}) collective-permute-start(bf16[512,256]{1,0:T(8,128)(2,1)} %get-tuple-element.174), channel_id=1, source_target_pairs={{0,4},{2,6},{4,8},{6,10},{8,12},{10,14},{12,16},{14,18},{16,20},{1... | collective-permute-start | bytes 786440 | tf_op jit(solution)/shard_map/ppermute | solution.py:15
  66.9 27.3 %copy-start.7 = (bf16[512,256]{1,0:T(8,128)(2,1)S(1)}, bf16[512,256]{1,0:T(8,128)(2,1)}, u32[]{:S(2)}) copy-start(bf16[512,256]{1,0:T(8,128)(2,1)} %param.18) | copy-start | bytes 786436
  100.3 12.8 %collective-permute-start.4 = (bf16[64,256]{1,0:T(8,128)(2,1)S(1)}, bf16[64,256]{1,0:T(8,128)(2,1)S(1)}, u32[]{:S(2)}, u32[]{:S(2)}) collective-permute-start(bf16[64,256]{1,0:T(8,128)(2,1)S(1)} %get-tuple-element.180), channel_id=1, source_target_pairs={{0,2},{2,4},{4,6},{6,8},{8,10},{10,12},{12,14},{14,16},{16,18},{18... | collective-permute-start | bytes 98312 | tf_op jit(solution)/shard_map/ppermute | solution.py:26
  102.8 10.3 %collective-permute-start.5 = (bf16[64,256]{1,0:T(8,128)(2,1)S(1)}, bf16[64,256]{1,0:T(8,128)(2,1)S(1)}, u32[]{:S(2)}, u32[]{:S(2)}) collective-permute-start(bf16[64,256]{1,0:T(8,128)(2,1)S(1)} %get-tuple-element.181), channel_id=1, source_target_pairs={{2,0},{4,2},{6,4},{8,6},{10,8},{12,10},{14,12},{16,14},{18,16},{20... | collective-permute-start | bytes 98312 | tf_op jit(solution)/shard_map/ppermute | solution.py:28
  127.7 5.7 %copy-start.1 = (bf16[2,4,512,256]{3,2,1,0:T(8,128)(2,1)S(1)}, bf16[2,4,512,256]{3,2,1,0:T(8,128)(2,1)}, u32[]{:S(2)}) copy-start(bf16[2,4,512,256]{3,2,1,0:T(8,128)(2,1)} %param.20) | copy-start | bytes 6291460
  136.5 11.9 %collective-permute-start.6 = (bf16[64,256]{1,0:T(8,128)(2,1)S(1)}, bf16[64,256]{1,0:T(8,128)(2,1)S(1)}, u32[]{:S(2)}, u32[]{:S(2)}) collective-permute-start(bf16[64,256]{1,0:T(8,128)(2,1)S(1)} %get-tuple-element.178), channel_id=1, source_target_pairs={{0,2},{2,4},{4,6},{6,8},{8,10},{10,12},{12,14},{14,16},{16,18},{18... | collective-permute-start | bytes 98312 | tf_op jit(solution)/shard_map/ppermute | solution.py:26
  138.5 10.0 %collective-permute-start.7 = (bf16[64,256]{1,0:T(8,128)(2,1)S(1)}, bf16[64,256]{1,0:T(8,128)(2,1)S(1)}, u32[]{:S(2)}, u32[]{:S(2)}) collective-permute-start(bf16[64,256]{1,0:T(8,128)(2,1)S(1)} %get-tuple-element.179), channel_id=1, source_target_pairs={{2,0},{4,2},{6,4},{8,6},{10,8},{12,10},{14,12},{16,14},{18,16},{20... | collective-permute-start | bytes 98312 | tf_op jit(solution)/shard_map/ppermute | solution.py:28
  163.1 6.0 %copy-start.3 = (f32[512,256]{1,0:T(8,128)S(1)}, f32[512,256]{1,0:T(8,128)}, u32[]{:S(2)}) copy-start(f32[512,256]{1,0:T(8,128)} %fusion.45) | copy-start | bytes 1572868
  169.2 15.4 %copy-start = (bf16[1024,512]{1,0:T(8,128)(2,1)S(1)}, bf16[1024,512]{1,0:T(8,128)(2,1)}, u32[]{:S(2)}) copy-start(bf16[1024,512]{1,0:T(8,128)(2,1)} %all-gather.3.cloned.1.call-done) | copy-start | bytes 3145732
  170.6 14.4 %copy-start.8 = (bf16[512,256]{1,0:T(8,128)(2,1)}, bf16[512,256]{1,0:T(8,128)(2,1)S(1)}, u32[]{:S(2)}) copy-start(bf16[512,256]{1,0:T(8,128)(2,1)S(1)} %add_convert_fusion.1) | copy-start | bytes 786436
  173.1 23.1 %collective-permute-start.8 = (bf16[512,256]{1,0:T(8,128)(2,1)S(1)}, bf16[512,256]{1,0:T(8,128)(2,1)S(1)}, u32[]{:S(2)}, u32[]{:S(2)}) collective-permute-start(bf16[512,256]{1,0:T(8,128)(2,1)S(1)} %convolution_convert_fusion.1), channel_id=1, source_target_pairs={{4,0},{6,2},{8,4},{10,6},{12,8},{14,10},{16,12},{18,14},{20,16},{2... | collective-permute-start | bytes 786440 | tf_op jit(solution)/shard_map/ppermute | solution.py:15
  178.3 24.7 %collective-permute-start.9 = (bf16[512,256]{1,0:T(8,128)(2,1)S(1)}, bf16[512,256]{1,0:T(8,128)(2,1)S(1)}, u32[]{:S(2)}, u32[]{:S(2)}) collective-permute-start(bf16[512,256]{1,0:T(8,128)(2,1)S(1)} %convolution_convert_fusion.1), channel_id=1, source_target_pairs={{2,0},{4,2},{6,4},{8,6},{10,8},{12,10},{14,12},{16,14},{18,16},{20... | collective-permute-start | bytes 786440 | tf_op jit(solution)/shard_map/ppermute | solution.py:15
  185.1 26.7 %collective-permute-start.10 = (bf16[512,256]{1,0:T(8,128)(2,1)S(1)}, bf16[512,256]{1,0:T(8,128)(2,1)S(1)}, u32[]{:S(2)}, u32[]{:S(2)}) collective-permute-start(bf16[512,256]{1,0:T(8,128)(2,1)S(1)} %convolution_convert_fusion.1), channel_id=1, source_target_pairs={{0,2},{2,4},{4,6},{6,8},{8,10},{10,12},{12,14},{14,16},{16,18},{18... | collective-permute-start | bytes 786440 | tf_op jit(solution)/shard_map/ppermute | solution.py:15
  187.5 29.0 %collective-permute-start.11 = (bf16[512,256]{1,0:T(8,128)(2,1)S(1)}, bf16[512,256]{1,0:T(8,128)(2,1)S(1)}, u32[]{:S(2)}, u32[]{:S(2)}) collective-permute-start(bf16[512,256]{1,0:T(8,128)(2,1)S(1)} %convolution_convert_fusion.1), channel_id=1, source_target_pairs={{0,4},{2,6},{4,8},{6,10},{8,12},{10,14},{12,16},{14,18},{16,20},{1... | collective-permute-start | bytes 786440 | tf_op jit(solution)/shard_map/ppermute | solution.py:15
  289.2 18.2 %copy-start.2 = (bf16[1024,256]{1,0:T(8,128)(2,1)S(1)}, bf16[1024,256]{1,0:T(8,128)(2,1)}, u32[]{:S(2)}) copy-start(bf16[1024,256]{1,0:T(8,128)(2,1)} %param.17) | copy-start | bytes 1572868
  (5 other events, 18.2 us)
Sparse Core Ops, SparseCore 0:
  9.8 16.2 all-gather.2
  291.5 15.9 all-gather.4
where the time goes:
time: 321 us; the launch traced here: 317 us
  local copies, waits for them, and re-layouts  103 us (32%)
  matrix products  56.5 us (18%)
  starting transfers between devices  53.8 us (17%)
  waiting for transfers between devices  41.2 us (13%)
  blocking collectives  19.2 us (6%)
  other arithmetic  18.7 us (6%)
  between operations  14.6 us (5%)
  loops' own time  10.2 us (3%)
    dot_general x15, matrix products, one_block(): lax.dot_general(one_hot, message, (((0,), (0,)), ((), ())), preferred_ele...  40.2 us
    ppermute x8, starting transfers between devices, from_behind(): lax.ppermute(value, axis, [(source, source + steps) for source in range(i...  32.2 us
    gather x2, local copies, waits for them, and re-layouts, mesh_messages(): extended[local_senders].astype(jnp.float32) + receiver_side[:, None, :]  29.2 us
    gather x15, local copies, waits for them, and re-layouts, one_block(): preact = picked.astype(jnp.float32) + receiver_side[targets_block]  23.6 us
    gather x5, local copies, waits for them, and re-layouts, band_pieces(): pieces.append(source_rows[senders[offset]])  22.8 us
    ppermute x2, starting transfers between devices, with_halo(): lax.ppermute(head, axis, [((i + 1) % count, i) for i in range(ends)])  17.1 us
    dot_general x16, matrix products, project(): return jnp.dot(latent, weights, preferred_element_type=jnp.float32)  16.2 us
    all_gather x1, waiting for transfers between devices, refresh(): lax.all_gather(summed.astype(jnp.bfloat16), 'feat', axis=1, tiled=True)  14.7 us
  transfers between devices with their start and end apart: 14, of which 5 were waited for; matrix products, arithmetic and copies ran while one was open for 11% of the time, Pallas kernels for 0%

commit v1 on v0

v1 whole, which is shorter than its diff:
```python
import functools

import jax
import jax.numpy as jnp
from jax import lax
from jax.experimental import pallas as pl
from jax.experimental.pallas import tpu as pltpu
from jax.sharding import PartitionSpec as P

REACH = 2
SPAN = 5
LAYERS = 2
MARGIN = 64
TILE = 256
F32 = jnp.float32
BF16 = jnp.bfloat16
VMEM_LIMIT = 40 * 1024 * 1024


def ring(value, steps):
    count = lax.axis_size("band")
    return lax.ppermute(value, "band", [(i, (i + steps) % count) for i in range(count)])


def swap(value):
    return lax.ppermute(value, "feat", [(0, 1), (1, 0)])


def silu(v):
    half = 0.5 * v
    return half + half * jnp.tanh(half)


def dot(a, b):
    return jnp.dot(a, b, preferred_element_type=F32)


def halves(feat):
    own = pl.ds(pl.multiple_of(feat * TILE, TILE), TILE)
    other = pl.ds(pl.multiple_of((1 - feat) * TILE, TILE), TILE)
    return own, other


def project(meta_ref, own, other, weights_ref):
    own_rows, other_rows = halves(meta_ref[0])
    return dot(own, weights_ref[own_rows, :]) + dot(other, weights_ref[other_rows, :])


def hot_columns(column, width):
    ids = lax.broadcasted_iota(jnp.int32, (column.shape[0], width), 1)
    return jnp.where(column == ids, 1.0, 0.0).astype(BF16)


def hot_rows(row, base, height):
    ids = lax.broadcasted_iota(jnp.int32, (height, row.shape[1]), 0) + base
    return jnp.where(row == ids, 1.0, 0.0).astype(BF16)


def call(kernel, name, operands, specs, outs, flops, scratch=()):
    size = sum(x.size * x.dtype.itemsize for x in outs)
    return pl.pallas_call(
        kernel,
        name=name,
        grid=(1,),
        in_specs=specs,
        out_specs=[whole(x) for x in outs],
        out_shape=list(outs),
        scratch_shapes=list(scratch),
        compiler_params=pltpu.CompilerParams(vmem_limit_bytes=VMEM_LIMIT),
        cost_estimate=pl.CostEstimate(flops=flops, bytes_accessed=2 * size, transcendentals=0),
    )(*operands)


def whole(x):
    return pl.BlockSpec(x.shape, lambda i, n=len(x.shape): (0,) * n)


def part(x, *index):
    lead = len(index)
    rest = x.shape[lead:]
    return pl.BlockSpec(
        (None,) * lead + rest, lambda i, where=index + (0,) * len(rest): where
    )


SMEM = pl.BlockSpec(memory_space=pltpu.SMEM)


def shape(rows, cols, dtype):
    return jax.ShapeDtypeStruct((rows, cols), dtype)


def encode_gather_kernel(meta, own, other, weights, senders, *refs):
    outs, sent = refs[:SPAN], refs[SPAN]
    for start in range(0, own.shape[0], TILE):
        rows = pl.ds(start, TILE)
        sent[rows, :] = project(meta, own[rows, :], other[rows, :], weights).astype(BF16)
    for offset in range(SPAN):
        for start in range(0, senders.shape[0], TILE):
            rows = pl.ds(start, TILE)
            hot = hot_columns(senders[rows, offset : offset + 1], sent.shape[0])
            outs[offset][rows, :] = dot(hot, sent[...]).astype(BF16)


def encode_gather(meta, own, other, weights, senders):
    slots = senders.shape[0]
    out = shape(slots, own.shape[1], BF16)
    return call(
        encode_gather_kernel,
        "encode_gather",
        (meta, own, other, weights, senders),
        [SMEM, whole(own), whole(other), part(weights, 0), whole(senders)],
        [out] * SPAN,
        2 * (SPAN * slots + 512) * own.shape[0] * own.shape[1],
        [pltpu.VMEM(own.shape, BF16)],
    )


def project_kernel(kinds, meta, own, other, *refs):
    count = len(kinds)
    for index in range(count):
        out = refs[count + index]
        for start in range(0, own.shape[0], TILE):
            rows = pl.ds(start, TILE)
            out[rows, :] = project(meta, own[rows, :], other[rows, :], refs[index]).astype(
                kinds[index]
            )


def projections(name, meta, own, other, picks, kinds):
    rows, cols = own.shape
    return call(
        functools.partial(project_kernel, kinds),
        name,
        (meta, own, other) + tuple(x for x, _ in picks),
        [SMEM, whole(own), whole(other)] + [part(x, *index) for x, index in picks],
        [shape(rows, cols, kind) for kind in kinds],
        2 * 512 * rows * cols * len(kinds),
    )


def bucket_step(rows_ref, recv_ref, sender_col, target_col, target_row, live_row, message):
    slots = target_col.shape[0]
    for start in range(0, slots, TILE):
        rows = slice(start, start + TILE)
        pre = dot(hot_columns(target_col[rows], recv_ref.shape[0]), recv_ref[...])
        if sender_col is None:
            pre = pre + rows_ref[rows, :].astype(F32)
        else:
            pre = pre + dot(hot_columns(sender_col[rows], rows_ref.shape[0]), rows_ref[...])
        message[rows, :] = silu(pre).astype(BF16)
    return jnp.where(live_row > 0, target_row, -1)


def bucket_kernel(offsets, gathers, has_total, *refs):
    count = len(offsets)
    pieces = refs[:count]
    rest = list(refs[count:])
    recv = rest.pop(0)
    total_in = rest.pop(0) if has_total else None
    senders = rest.pop(0) if gathers else None
    target_cols, target_rows, live_rows, out, total, message = rest
    nodes = recv.shape[0]
    for index, offset in enumerate(offsets):
        pick = slice(offset, offset + 1)
        where = bucket_step(
            pieces[index],
            recv,
            senders[:, pick] if gathers else None,
            target_cols[:, pick],
            target_rows[pick, :],
            live_rows[pick, :],
            message,
        )
        for start in range(0, nodes, TILE):
            rows = pl.ds(start, TILE)
            value = dot(hot_rows(where, start, TILE), message[...])
            if index > 0:
                value = value + total[rows, :]
            elif has_total:
                value = value + total_in[rows, :]
            if index == count - 1:
                out[rows, :] = value.astype(out.dtype)
            else:
                total[rows, :] = value


def buckets(name, offsets, pieces, recv, total, senders, target_cols, target_rows, live_rows, kind):
    nodes, cols = recv.shape
    slots = target_rows.shape[1]
    operands = list(pieces) + [recv]
    if total is not None:
        operands.append(total)
    if senders is not None:
        operands.append(senders)
    operands += [target_cols, target_rows, live_rows]
    return call(
        functools.partial(bucket_kernel, offsets, senders is not None, total is not None),
        name,
        operands,
        [whole(x) for x in operands],
        [shape(nodes, cols, kind)],
        2 * len(offsets) * slots * cols * (2 * nodes + (512 if senders is not None else 0)),
        [pltpu.VMEM((nodes, cols), F32), pltpu.VMEM((slots, cols), BF16)],
    )[0]


def update_kernel(last, meta, own, other, sum_own, sum_other, w2, w3, w2_other, w3_other, w0, *outs):
    total = own.shape[0]
    for start in range(0, total, TILE):
        rows = pl.ds(start, TILE)
        a, b, c, d = own[rows, :], other[rows, :], sum_own[rows, :], sum_other[rows, :]
        first = project(meta, a, b, w2) + project(meta, c, d, w3)
        outs[0][rows, :] = (a.astype(F32) + silu(first)).astype(BF16)
        second = project(meta, a, b, w2_other) + project(meta, c, d, w3_other)
        outs[1][rows, :] = (b.astype(F32) + silu(second)).astype(BF16)
    now_own, now_other = outs[0], outs[1]
    if last:
        for start in range(0, total, TILE):
            rows = pl.ds(start, TILE)
            outs[2][rows, :] = project(meta, now_own[rows, :], now_other[rows, :], w0).astype(BF16)
    else:
        for out, start in ((outs[2], 0), (outs[3], total - MARGIN)):
            rows = pl.ds(start, MARGIN)
            out[...] = project(meta, now_own[rows, :], now_other[rows, :], w0).astype(BF16)


def update(name, meta, own, other, sum_own, sum_other, w, w_other, where, w0, where0, last):
    rows, cols = own.shape
    full = shape(rows, cols, BF16)
    edge = shape(MARGIN, cols, BF16)
    operands = (meta, own, other, sum_own, sum_other, w, w, w_other, w_other, w0)
    specs = [SMEM] + [whole(x) for x in operands[1:5]]
    specs += [part(w, *where, 2), part(w, *where, 3)]
    specs += [part(w_other, *where, 2), part(w_other, *where, 3), part(w0, *where0)]
    return call(
        functools.partial(update_kernel, last),
        name,
        operands,
        specs,
        [full] * 3 if last else [full, full, edge, edge],
        2 * rows * cols * 512 * 5,
    )


def mesh_kernel(meta, sent, recv, before, after, senders, live, out, extended):
    rows_total = sent.shape[0]
    extended[0:MARGIN, :] = before[...]
    extended[MARGIN : MARGIN + rows_total, :] = sent[...]
    extended[MARGIN + rows_total :, :] = after[...]
    base = meta[1] * rows_total - MARGIN
    for start in range(0, rows_total, TILE):
        rows = pl.ds(start, TILE)
        side = recv[rows, :]
        local = senders[rows, :] - base
        flags = live[rows, :].astype(F32)
        total = jnp.zeros(side.shape, F32)
        for k in range(senders.shape[1]):
            hot = hot_columns(local[:, k : k + 1], extended.shape[0])
            message = silu(dot(hot, extended[...]) + side) * flags[:, k : k + 1]
            total = total + message.astype(BF16).astype(F32)
        out[rows, :] = total.astype(BF16)


def mesh_messages(name, meta, sent, recv, before, after, senders, live):
    rows, cols = sent.shape
    operands = (meta, sent, recv, before, after, senders, live)
    return call(
        mesh_kernel,
        name,
        operands,
        [SMEM] + [whole(x) for x in operands[1:]],
        [shape(rows, cols, BF16)],
        2 * rows * senders.shape[1] * (rows + 2 * MARGIN) * cols,
        [pltpu.VMEM((rows + 2 * MARGIN, cols), BF16)],
    )[0]


def final_kernel(meta, own, self_term, sum_own, sum_other, w3, out):
    for start in range(0, own.shape[0], TILE):
        rows = pl.ds(start, TILE)
        term = self_term[rows, :] + project(meta, sum_own[rows, :], sum_other[rows, :], w3)
        out[rows, :] = (own[rows, :].astype(F32) + silu(term)).astype(BF16)


def body(
    grid_latent,
    mesh_latent,
    encode_weights,
    layer_weights,
    decode_weights,
    encode_senders,
    encode_targets,
    encode_live,
    mesh_senders,
    mesh_live,
    decode_senders,
    decode_targets,
    decode_live,
):
    meta = jnp.stack([lax.axis_index("feat"), lax.axis_index("band")]).astype(jnp.int32)
    grid_other = swap(grid_latent)
    mesh_other = swap(mesh_latent)
    encode_other = swap(encode_weights)
    layer_other = swap(layer_weights)

    pieces = encode_gather(meta, grid_latent, grid_other, encode_weights, encode_senders[0].T)
    arrived = [x if o == REACH else ring(x, o - REACH) for o, x in enumerate(pieces)]
    (encode_recv,) = projections(
        "encode_recv", meta, mesh_latent, mesh_other, [(encode_weights, (1,))], [BF16]
    )
    targets = encode_targets[0]
    slots = (targets.T, targets, encode_live[0])
    total = buckets(
        "encode_own", (REACH,), [arrived[REACH]], encode_recv, None, None, *slots, F32
    )
    decode_recv, grid_self = projections(
        "decode_recv",
        meta,
        grid_latent,
        grid_other,
        [(decode_weights, (1,)), (decode_weights, (2,))],
        [BF16, F32],
    )
    encode_sum = buckets(
        "encode_rest",
        (0, 1, 3, 4),
        [arrived[o] for o in (0, 1, 3, 4)],
        encode_recv,
        total,
        None,
        *slots,
        BF16,
    )
    own, other, head, tail = update(
        "encode_update",
        meta,
        mesh_latent,
        mesh_other,
        encode_sum,
        swap(encode_sum),
        encode_weights,
        encode_other,
        (),
        layer_weights,
        (0, 0),
        False,
    )
    for layer in range(LAYERS):
        before = ring(tail, 1)
        after = ring(head, -1)
        sent, recv = projections(
            f"layer_project_{layer}",
            meta,
            own,
            other,
            [(layer_weights, (layer, 0)), (layer_weights, (layer, 1))],
            [BF16, F32],
        )
        summed = mesh_messages(
            f"layer_messages_{layer}", meta, sent, recv, before, after, mesh_senders, mesh_live
        )
        last = layer == LAYERS - 1
        results = update(
            f"layer_update_{layer}",
            meta,
            own,
            other,
            summed,
            swap(summed),
            layer_weights,
            layer_other,
            (layer,),
            decode_weights if last else layer_weights,
            (0,) if last else (layer + 1, 0),
            last,
        )
        own, other = results[0], results[1]
        if last:
            decode_sent = results[2]
        else:
            head, tail = results[2], results[3]

    targets = decode_targets[0]
    slots = (decode_senders[0].T, targets.T, targets, decode_live[0])
    rows = [decode_sent if o == REACH else ring(decode_sent, o - REACH) for o in range(SPAN)]
    total = buckets("decode_own", (2,), [rows[2]], decode_recv, None, *slots, F32)
    total = buckets("decode_near", (1, 3), [rows[1], rows[3]], decode_recv, total, *slots, F32)
    decode_sum = buckets("decode_far", (0, 4), [rows[0], rows[4]], decode_recv, total, *slots, BF16)
    decode_other = swap(decode_sum)
    operands = (meta, grid_latent, grid_self, decode_sum, decode_other, decode_weights)
    (grid_now,) = call(
        final_kernel,
        "final_update",
        operands,
        [SMEM] + [whole(x) for x in operands[1:5]] + [part(decode_weights, 3)],
        [shape(*grid_latent.shape, BF16)],
        2 * 512 * grid_latent.size,
    )
    return own, grid_now


def solution(mesh):
    placed = (
        P("band", "feat"),
        P("band", "feat"),
        P(None, None, "feat"),
        P(None, None, None, "feat"),
        P(None, None, "feat"),
        P("band", None, None),
        P("band", None, None),
        P("band", None, None),
        P("band", None),
        P("band", None),
        P("band", None, None),
        P("band", None, None),
        P("band", None, None),
    )
    return jax.shard_map(
        body,
        mesh=mesh,
        in_specs=placed,
        out_specs=(P("band", "feat"), P("band", "feat")),
        check_vma=False,
    )
```

time: 321 us -> 125 us (0.39)
  the two profiles are of different devices: /device:TPU:129 before, /device:TPU:3 now
where the time goes in v1:
time: 125 us; the launch traced here: 124 us
  starting transfers between devices  47.7 us (38%)
  Pallas kernels  35.5 us (28%)
  waiting for transfers between devices  31.3 us (25%)
  local copies, waits for them, and re-layouts  8.78 us (7%)
    ppermute x12, starting transfers between devices, ring(): lax.ppermute(value, 'band', [(i, (i + steps) % count) for i in range(coun...  39.7 us
    pallas_call x16, Pallas kernels, call(): pl.pallas_call(kernel, name=name, grid=(1,), in_specs=specs, out_specs=[w...  35.5 us
    ppermute x12, waiting for transfers between devices, ring(): lax.ppermute(value, 'band', [(i, (i + steps) % count) for i in range(coun...  22.4 us
    ppermute x8, waiting for transfers between devices, swap(): return lax.ppermute(value, 'feat', [(0, 1), (1, 0)])  8.86 us
    unnamed x64, local copies, waits for them, and re-layouts  8.41 us
    ppermute x8, starting transfers between devices, swap(): return lax.ppermute(value, 'feat', [(0, 1), (1, 0)])  8.02 us
  transfers between devices with their start and end apart: 20, of which 10 were waited for; matrix products, arithmetic and copies ran while one was open for 1% of the time, Pallas kernels for 18%

profile of v1, /device:TPU:3, one launch (start us, length us, event | category | flops | bytes accessed | tf_op | source)
XLA Modules:
  0.0 124.4 jit_solution(14110674023161522558)
XLA Ops:
  2.9 3.8 %collective-permute-done.1.other = bf16[1024,256]{1,0:T(8,128)(2,1)S(1)} collective-permute-done((bf16[1024,256]{1,0:T(8,128)(2,1)}, bf16[1024,256]{1,0:T(8,128)(2,1)S(1)}, u32[]{:S(2)}, u32[]{:S(2)}) %collective-permute-start.1) | collective-permute-done | bytes 524320 | tf_op jit(solution)/shard_map/ppermute | solution.py:26
  9.2 3.1 %encode_gather.1 = (bf16[512,256]{1,0:T(8,128)(2,1)S(1)}, bf16[512,256]{1,0:T(8,128)(2,1)}, bf16[512,256]{1,0:T(8,128)(2,1)S(1)}, bf16[512,256]{1,0:T(8,128)(2,1)}, bf16[512,256]{1,0:T(8,128)(2,1)}) custom-call(s32[2]{0:T(128)S(1)} %pad_add_fusion.meta, bf16[1024,256]{1,0:T(8,128)(2,1)S(1)} %copy-done.4, bf16[1024,256]{1,0:T(8,128)(2,1)S(1)} %collective-permute-done.1.other, ...), custom_call_target="tpu_custom_call" | custom-call | flops 1610612736 | bytes 2621440 | tf_op jit(solution)/shard_map/encode_gather/pallas_call | solution.py:61
  12.3 9.6 %collective-permute-start.2 = (bf16[512,256]{1,0:T(8,128)(2,1)S(1)}, bf16[512,256]{1,0:T(8,128)(2,1)S(1)}, u32[]{:S(2)}, u32[]{:S(2)}) collective-permute-start(bf16[512,256]{1,0:T(8,128)(2,1)S(1)} %get-tuple-element.23), channel_id=1, source_target_pairs={{0,252},{2,254},{4,0},{6,2},{8,4},{10,6},{12,8},{14,10},{16,12},{1... | collective-permute-start | bytes 786440 | tf_op jit(solution)/shard_map/ppermute | solution.py:22
  23.4 4.1 %collective-permute-done.2.refs_0_ = bf16[512,256]{1,0:T(8,128)(2,1)S(1)} collective-permute-done((bf16[512,256]{1,0:T(8,128)(2,1)S(1)}, bf16[512,256]{1,0:T(8,128)(2,1)S(1)}, u32[]{:S(2)}, u32[]{:S(2)}) %collective-permute-start.2) | collective-permute-done | bytes 262176 | tf_op jit(solution)/shard_map/ppermute | solution.py:22
  30.0 5.2 %collective-permute-done.3.refs_1_ = bf16[512,256]{1,0:T(8,128)(2,1)} collective-permute-done((bf16[512,256]{1,0:T(8,128)(2,1)}, bf16[512,256]{1,0:T(8,128)(2,1)}, u32[]{:S(2)}, u32[]{:S(2)}) %collective-permute-start.3) | collective-permute-done | bytes 262176 | tf_op jit(solution)/shard_map/ppermute | solution.py:22
  35.3 6.5 %collective-permute-done.5.refs_3_ = bf16[512,256]{1,0:T(8,128)(2,1)} collective-permute-done((bf16[512,256]{1,0:T(8,128)(2,1)}, bf16[512,256]{1,0:T(8,128)(2,1)}, u32[]{:S(2)}, u32[]{:S(2)}) %collective-permute-start.5) | collective-permute-done | bytes 262176 | tf_op jit(solution)/shard_map/ppermute | solution.py:22
  41.7 3.2 %encode_rest.1.sum_own = bf16[512,256]{1,0:T(8,128)(2,1)S(1)} custom-call(bf16[512,256]{1,0:T(8,128)(2,1)S(1)} %copy-done.20, bf16[512,256]{1,0:T(8,128)(2,1)} %collective-permute-done.3.refs_1_, bf16[512,256]{1,0:T(8,128)(2,1)} %collective-permute-done.4.refs_2_, bf16[512,256]{1,0:T(8,128)(2,1)} %collective-permute-done.5.refs_3_, ...), custom_call_target="tpu_custom_call" | custom-call | flops 1073741824 | bytes 524288 | tf_op jit(solution)/shard_map/encode_rest/pallas_call | solution.py:61
  45.0 2.1 %collective-permute-start.6 = (bf16[512,256]{1,0:T(8,128)(2,1)S(1)}, bf16[512,256]{1,0:T(8,128)(2,1)S(1)}, u32[]{:S(2)}, u32[]{:S(2)}) collective-permute-start(bf16[512,256]{1,0:T(8,128)(2,1)S(1)} %encode_rest.1.sum_own), channel_id=1, source_target_pairs={{0,1},{1,0},{2,3},{3,2},{4,5},{5,4},{6,7},{7,6},{8,9},{9,8},{10,11... | collective-permute-start | bytes 786440 | tf_op jit(solution)/shard_map/ppermute | solution.py:26
  48.2 2.1 %encode_update.1 = (bf16[512,256]{1,0:T(8,128)(2,1)S(1)}, bf16[512,256]{1,0:T(8,128)(2,1)S(1)}, bf16[64,256]{1,0:T(8,128)(2,1)S(1)}, bf16[64,256]{1,0:T(8,128)(2,1)S(1)}) custom-call(s32[2]{0:T(128)S(1)} %pad_add_fusion.meta, bf16[512,256]{1,0:T(8,128)(2,1)S(1)} %copy-done.10, bf16[512,256]{1,0:T(8,128)(2,1)S(1)} %copy-done.12, ...), custom_call_target="tpu_custom_call" | custom-call | flops 671088640 | bytes 1179648 | tf_op jit(solution)/shard_map/encode_update/pallas_call | solution.py:61
  51.0 1.5 %collective-permute-start.9 = (bf16[64,256]{1,0:T(8,128)(2,1)S(1)}, bf16[64,256]{1,0:T(8,128)(2,1)S(1)}, u32[]{:S(2)}, u32[]{:S(2)}) collective-permute-start(bf16[64,256]{1,0:T(8,128)(2,1)S(1)} %get-tuple-element.33), channel_id=1, source_target_pairs={{0,254},{2,0},{4,2},{6,4},{8,6},{10,8},{12,10},{14,12},{16,14},{18... | collective-permute-start | bytes 98312 | tf_op jit(solution)/shard_map/ppermute | solution.py:22
  54.9 3.3 %layer_messages_0.1.sum_own = bf16[512,256]{1,0:T(8,128)(2,1)S(1)} custom-call(s32[2]{0:T(128)S(1)} %pad_add_fusion.meta, bf16[512,256]{1,0:T(8,128)(2,1)S(1)} %get-tuple-element.30.sent, f32[512,256]{1,0:T(8,128)S(1)} %get-tuple-element.31.recv, bf16[64,256]{1,0:T(8,128)(2,1)S(1)} %collective-permute-done.8.before, ...), custom_call_target="tpu_custom_call" | custom-call | flops 1342177280 | bytes 524288 | tf_op jit(solution)/shard_map/layer_messages_0/pallas_call | solution.py:61
  60.3 2.1 %layer_update_0.1 = (bf16[512,256]{1,0:T(8,128)(2,1)S(1)}, bf16[512,256]{1,0:T(8,128)(2,1)S(1)}, bf16[64,256]{1,0:T(8,128)(2,1)S(1)}, bf16[64,256]{1,0:T(8,128)(2,1)S(1)}) custom-call(s32[2]{0:T(128)S(1)} %pad_add_fusion.meta, bf16[512,256]{1,0:T(8,128)(2,1)S(1)} %get-tuple-element.28.own, bf16[512,256]{1,0:T(8,128)(2,1)S(1)} %copy-done.8, ...), custom_call_target="tpu_custom_call" | custom-call | flops 671088640 | bytes 1179648 | tf_op jit(solution)/shard_map/layer_update_0/pallas_call | solution.py:61
  62.5 6.7 %collective-permute-start.13 = (bf16[64,256]{1,0:T(8,128)(2,1)S(1)}, bf16[64,256]{1,0:T(8,128)(2,1)S(1)}, u32[]{:S(2)}, u32[]{:S(2)}) collective-permute-start(bf16[64,256]{1,0:T(8,128)(2,1)S(1)} %get-tuple-element.39), channel_id=1, source_target_pairs={{0,254},{2,0},{4,2},{6,4},{8,6},{10,8},{12,10},{14,12},{16,14},{18... | collective-permute-start | bytes 98312 | tf_op jit(solution)/shard_map/ppermute | solution.py:22
  70.4 3.3 %layer_messages_1.1.sum_own = bf16[512,256]{1,0:T(8,128)(2,1)S(1)} custom-call(s32[2]{0:T(128)S(1)} %pad_add_fusion.meta, bf16[512,256]{1,0:T(8,128)(2,1)S(1)} %get-tuple-element.36.sent, f32[512,256]{1,0:T(8,128)S(1)} %get-tuple-element.37.recv, bf16[64,256]{1,0:T(8,128)(2,1)S(1)} %collective-permute-done.12.before, ...), custom_call_target="tpu_custom_call" | custom-call | flops 1342177280 | bytes 524288 | tf_op jit(solution)/shard_map/layer_messages_1/pallas_call | solution.py:61
  76.2 2.7 %layer_update_1.1 = (bf16[512,256]{1,0:T(8,128)(2,1)}, bf16[512,256]{1,0:T(8,128)(2,1)}, bf16[512,256]{1,0:T(8,128)(2,1)S(1)}) custom-call(s32[2]{0:T(128)S(1)} %pad_add_fusion.meta, bf16[512,256]{1,0:T(8,128)(2,1)S(1)} %get-tuple-element.34.own, bf16[512,256]{1,0:T(8,128)(2,1)S(1)} %get-tuple-element.35.other, ...), custom_call_target="tpu_custom_call" | custom-call | flops 671088640 | bytes 1572864 | tf_op jit(solution)/shard_map/layer_update_1/pallas_call | solution.py:61
  78.9 7.2 %collective-permute-start.17 = (bf16[512,256]{1,0:T(8,128)(2,1)S(1)}, bf16[512,256]{1,0:T(8,128)(2,1)S(1)}, u32[]{:S(2)}, u32[]{:S(2)}) collective-permute-start(bf16[512,256]{1,0:T(8,128)(2,1)S(1)} %get-tuple-element.42.refs_0_), channel_id=1, source_target_pairs={{0,254},{2,0},{4,2},{6,4},{8,6},{10,8},{12,10},{14,12},{16,14},{18... | collective-permute-start | bytes 786440 | tf_op jit(solution)/shard_map/ppermute | solution.py:22
  90.0 13.2 %collective-permute-start.15 = (bf16[512,256]{1,0:T(8,128)(2,1)S(1)}, bf16[512,256]{1,0:T(8,128)(2,1)S(1)}, u32[]{:S(2)}, u32[]{:S(2)}) collective-permute-start(bf16[512,256]{1,0:T(8,128)(2,1)S(1)} %get-tuple-element.42.refs_0_), channel_id=1, source_target_pairs={{0,252},{2,254},{4,0},{6,2},{8,4},{10,6},{12,8},{14,10},{16,12},{1... | collective-permute-start | bytes 786440 | tf_op jit(solution)/shard_map/ppermute | solution.py:22
  103.2 1.8 %decode_own.1.refs_3_ = f32[1024,256]{1,0:T(8,128)S(1)} custom-call(bf16[512,256]{1,0:T(8,128)(2,1)S(1)} %get-tuple-element.42.refs_0_, bf16[1024,256]{1,0:T(8,128)(2,1)S(1)} %get-tuple-element.43.refs_1_.refs_2_, s32[1024,5]{1,0:T(8,128)S(1)} %bitcast.31, s32[1024,5]{1,0:T(8,128)S(1)} %bitcast.28, s32[5,1024]{1,0:T(8,128)S(1)} %bitcast.39, ...), custom_call_target="tpu_custom_call" | custom-call | flops 1342177280 | bytes 2097152 | tf_op jit(solution)/shard_map/decode_own/pallas_call | solution.py:61
  105.0 4.2 %decode_near.1.refs_3_ = f32[1024,256]{1,0:T(8,128)S(1)} custom-call(bf16[512,256]{1,0:T(8,128)(2,1)S(1)} %collective-permute-done.17.refs_0_, bf16[512,256]{1,0:T(8,128)(2,1)} %collective-permute-done.18.refs_1_, bf16[1024,256]{1,0:T(8,128)(2,1)S(1)} %get-tuple-element.43.refs_1_.refs_2_, f32[1024,256]{1,0:T(8,128)S(1)} %decode_own.1.refs_3_, ...), custom_call_target="tpu_custom_call" | custom-call | flops 2684354560 | bytes 2097152 | tf_op jit(solution)/shard_map/decode_near/pallas_call | solution.py:61
  109.2 6.3 %collective-permute-done.16.refs_1_ = bf16[512,256]{1,0:T(8,128)(2,1)S(1)} collective-permute-done((bf16[512,256]{1,0:T(8,128)(2,1)S(1)}, bf16[512,256]{1,0:T(8,128)(2,1)S(1)}, u32[]{:S(2)}, u32[]{:S(2)}) %collective-permute-start.16) | collective-permute-done | bytes 262176 | tf_op jit(solution)/shard_map/ppermute | solution.py:22
  115.5 3.2 %decode_far.1.sum_own = bf16[1024,256]{1,0:T(8,128)(2,1)S(1)} custom-call(bf16[512,256]{1,0:T(8,128)(2,1)S(1)} %collective-permute-done.15.refs_0_, bf16[512,256]{1,0:T(8,128)(2,1)S(1)} %collective-permute-done.16.refs_1_, bf16[1024,256]{1,0:T(8,128)(2,1)S(1)} %get-tuple-element.43.refs_1_.refs_2_, f32[1024,256]{1,0:T(8,128)S(1)} %decode_near.1.refs_3_, ...), custom_call_target="tpu_custom_call" | custom-call | flops 2684354560 | bytes 1048576 | tf_op jit(solution)/shard_map/decode_far/pallas_call | solution.py:61
  118.7 2.2 %collective-permute-start.19 = (bf16[1024,256]{1,0:T(8,128)(2,1)S(1)}, bf16[1024,256]{1,0:T(8,128)(2,1)S(1)}, u32[]{:S(2)}, u32[]{:S(2)}) collective-permute-start(bf16[1024,256]{1,0:T(8,128)(2,1)S(1)} %decode_far.1.sum_own), channel_id=1, source_target_pairs={{0,1},{1,0},{2,3},{3,2},{4,5},{5,4},{6,7},{7,6},{8,9},{9,8},{10,11... | collective-permute-start | bytes 1572872 | tf_op jit(solution)/shard_map/ppermute | solution.py:26
  121.0 1.5 %collective-permute-done.19.sum_other = bf16[1024,256]{1,0:T(8,128)(2,1)S(1)} collective-permute-done((bf16[1024,256]{1,0:T(8,128)(2,1)S(1)}, bf16[1024,256]{1,0:T(8,128)(2,1)S(1)}, u32[]{:S(2)}, u32[]{:S(2)}) %collective-permute-start.19) | collective-permute-done | bytes 524320 | tf_op jit(solution)/shard_map/ppermute | solution.py:26
  122.5 1.9 %final_update.1 = bf16[1024,256]{1,0:T(8,128)(2,1)} custom-call(s32[2]{0:T(128)S(1)} %pad_add_fusion.meta, bf16[1024,256]{1,0:T(8,128)(2,1)S(1)} %copy-done.6, f32[1024,256]{1,0:T(8,128)S(1)} %get-tuple-element.41.self_term, bf16[1024,256]{1,0:T(8,128)(2,1)S(1)} %decode_far.1.sum_own, bf16[1024,256]{1,0:T(8,128)(2,1)S(1)} %collective-permute-done.19.sum_other, ...), custom_call_target="tpu_custom_call" | custom-call | flops 268435456 | bytes 1048576 | tf_op jit(solution)/shard_map/final_update/pallas_call | solution.py:61
  (99 shorter events, 22.6 us)
Async XLA Ops:
  0.6 59.7 %collective-permute-start.11 = (bf16[2,4,512,256]{3,2,1,0:T(8,128)(2,1)}, bf16[2,4,512,256]{3,2,1,0:T(8,128)(2,1)}, u32[]{:S(2)}, u32[]{:S(2)}) collective-permute-start(bf16[2,4,512,256]{3,2,1,0:T(8,128)(2,1)} %w3.6), channel_id=1, source_target_pairs={{0,1},{1,0},{2,3},{3,2},{4,5},{5,4},{6,7},{7,6},{8,9},{9,8},{10,11... | collective-permute-start | bytes 6291464 | tf_op jit(solution)/shard_map/ppermute | solution.py:26
  1.4 5.4 %collective-permute-start.1 = (bf16[1024,256]{1,0:T(8,128)(2,1)}, bf16[1024,256]{1,0:T(8,128)(2,1)S(1)}, u32[]{:S(2)}, u32[]{:S(2)}) collective-permute-start(bf16[1024,256]{1,0:T(8,128)(2,1)} %own.9), channel_id=1, source_target_pairs={{0,1},{1,0},{2,3},{3,2},{4,5},{5,4},{6,7},{7,6},{8,9},{9,8},{10,11... | collective-permute-start | bytes 1572872 | tf_op jit(solution)/shard_map/ppermute | solution.py:26
  1.5 21.5 %collective-permute-start = (bf16[512,256]{1,0:T(8,128)(2,1)}, bf16[512,256]{1,0:T(8,128)(2,1)S(1)}, u32[]{:S(2)}, u32[]{:S(2)}) collective-permute-start(bf16[512,256]{1,0:T(8,128)(2,1)} %own.7), channel_id=1, source_target_pairs={{0,1},{1,0},{2,3},{3,2},{4,5},{5,4},{6,7},{7,6},{8,9},{9,8},{10,11... | collective-permute-start | bytes 786440 | tf_op jit(solution)/shard_map/ppermute | solution.py:26
  1.9 46.3 %collective-permute-start.7 = (bf16[4,512,256]{2,1,0:T(8,128)(2,1)}, bf16[4,512,256]{2,1,0:T(8,128)(2,1)}, u32[]{:S(2)}, u32[]{:S(2)}) collective-permute-start(bf16[4,512,256]{2,1,0:T(8,128)(2,1)} %w3.4), channel_id=1, source_target_pairs={{0,1},{1,0},{2,3},{3,2},{4,5},{5,4},{6,7},{7,6},{8,9},{9,8},{10,11... | collective-permute-start | bytes 3145736 | tf_op jit(solution)/shard_map/ppermute | solution.py:26
  9.2 19.0 %copy-start.22 = (s32[1,5,512]{2,0,1:T(1,128)S(1)}, s32[1,5,512]{2,0,1:T(1,128)}, u32[]{:S(2)}) copy-start(s32[1,5,512]{2,0,1:T(1,128)} %param.19) | copy-start | bytes 30724
  9.2 19.2 %copy-start.27 = (s32[1,5,512]{2,0,1:T(1,128)S(1)}, s32[1,5,512]{2,0,1:T(1,128)}, u32[]{:S(2)}) copy-start(s32[1,5,512]{2,0,1:T(1,128)} %param.20) | copy-start | bytes 30724
  9.2 19.2 %copy-start.3 = (bf16[4,512,256]{2,1,0:T(8,128)(2,1)S(1)}, bf16[4,512,256]{2,1,0:T(8,128)(2,1)}, u32[]{:S(2)}) copy-start(bf16[4,512,256]{2,1,0:T(8,128)(2,1)} %w3.4) | copy-start | bytes 3145732
  9.2 19.2 %copy-start.9 = (bf16[512,256]{1,0:T(8,128)(2,1)S(1)}, bf16[512,256]{1,0:T(8,128)(2,1)}, u32[]{:S(2)}) copy-start(bf16[512,256]{1,0:T(8,128)(2,1)} %own.7) | copy-start | bytes 786436
  12.3 15.2 %collective-permute-start.2 = (bf16[512,256]{1,0:T(8,128)(2,1)S(1)}, bf16[512,256]{1,0:T(8,128)(2,1)S(1)}, u32[]{:S(2)}, u32[]{:S(2)}) collective-permute-start(bf16[512,256]{1,0:T(8,128)(2,1)S(1)} %get-tuple-element.23), channel_id=1, source_target_pairs={{0,252},{2,254},{4,0},{6,2},{8,4},{10,6},{12,8},{14,10},{16,12},{1... | collective-permute-start | bytes 786440 | tf_op jit(solution)/shard_map/ppermute | solution.py:22
  21.9 13.4 %collective-permute-start.3 = (bf16[512,256]{1,0:T(8,128)(2,1)}, bf16[512,256]{1,0:T(8,128)(2,1)}, u32[]{:S(2)}, u32[]{:S(2)}) collective-permute-start(bf16[512,256]{1,0:T(8,128)(2,1)} %get-tuple-element.24), channel_id=1, source_target_pairs={{0,254},{2,0},{4,2},{6,4},{8,6},{10,8},{12,10},{14,12},{16,14},{18... | collective-permute-start | bytes 786440 | tf_op jit(solution)/shard_map/ppermute | solution.py:22
  23.0 12.2 %collective-permute-start.4 = (bf16[512,256]{1,0:T(8,128)(2,1)}, bf16[512,256]{1,0:T(8,128)(2,1)}, u32[]{:S(2)}, u32[]{:S(2)}) collective-permute-start(bf16[512,256]{1,0:T(8,128)(2,1)} %get-tuple-element.25), channel_id=1, source_target_pairs={{0,2},{2,4},{4,6},{6,8},{8,10},{10,12},{12,14},{14,16},{16,18},{18... | collective-permute-start | bytes 786440 | tf_op jit(solution)/shard_map/ppermute | solution.py:22
  28.2 13.5 %collective-permute-start.5 = (bf16[512,256]{1,0:T(8,128)(2,1)}, bf16[512,256]{1,0:T(8,128)(2,1)}, u32[]{:S(2)}, u32[]{:S(2)}) collective-permute-start(bf16[512,256]{1,0:T(8,128)(2,1)} %get-tuple-element.26), channel_id=1, source_target_pairs={{0,4},{2,6},{4,8},{6,10},{8,12},{10,14},{12,16},{14,18},{16,20},{1... | collective-permute-start | bytes 786440 | tf_op jit(solution)/shard_map/ppermute | solution.py:22
  45.0 3.2 %collective-permute-start.6 = (bf16[512,256]{1,0:T(8,128)(2,1)S(1)}, bf16[512,256]{1,0:T(8,128)(2,1)S(1)}, u32[]{:S(2)}, u32[]{:S(2)}) collective-permute-start(bf16[512,256]{1,0:T(8,128)(2,1)S(1)} %encode_rest.1.sum_own), channel_id=1, source_target_pairs={{0,1},{1,0},{2,3},{3,2},{4,5},{5,4},{6,7},{7,6},{8,9},{9,8},{10,11... | collective-permute-start | bytes 786440 | tf_op jit(solution)/shard_map/ppermute | solution.py:26
  51.0 3.8 %collective-permute-start.8 = (bf16[64,256]{1,0:T(8,128)(2,1)S(1)}, bf16[64,256]{1,0:T(8,128)(2,1)S(1)}, u32[]{:S(2)}, u32[]{:S(2)}) collective-permute-start(bf16[64,256]{1,0:T(8,128)(2,1)S(1)} %get-tuple-element.32), channel_id=1, source_target_pairs={{0,2},{2,4},{4,6},{6,8},{8,10},{10,12},{12,14},{14,16},{16,18},{18... | collective-permute-start | bytes 98312 | tf_op jit(solution)/shard_map/ppermute | solution.py:22
  51.0 3.8 %collective-permute-start.9 = (bf16[64,256]{1,0:T(8,128)(2,1)S(1)}, bf16[64,256]{1,0:T(8,128)(2,1)S(1)}, u32[]{:S(2)}, u32[]{:S(2)}) collective-permute-start(bf16[64,256]{1,0:T(8,128)(2,1)S(1)} %get-tuple-element.33), channel_id=1, source_target_pairs={{0,254},{2,0},{4,2},{6,4},{8,6},{10,8},{12,10},{14,12},{16,14},{18... | collective-permute-start | bytes 98312 | tf_op jit(solution)/shard_map/ppermute | solution.py:22
  58.1 2.2 %collective-permute-start.10 = (bf16[512,256]{1,0:T(8,128)(2,1)S(1)}, bf16[512,256]{1,0:T(8,128)(2,1)S(1)}, u32[]{:S(2)}, u32[]{:S(2)}) collective-permute-start(bf16[512,256]{1,0:T(8,128)(2,1)S(1)} %layer_messages_0.1.sum_own), channel_id=1, source_target_pairs={{0,1},{1,0},{2,3},{3,2},{4,5},{5,4},{6,7},{7,6},{8,9},{9,8},{10,11... | collective-permute-start | bytes 786440 | tf_op jit(solution)/shard_map/ppermute | solution.py:26
  62.4 8.0 %collective-permute-start.12 = (bf16[64,256]{1,0:T(8,128)(2,1)S(1)}, bf16[64,256]{1,0:T(8,128)(2,1)S(1)}, u32[]{:S(2)}, u32[]{:S(2)}) collective-permute-start(bf16[64,256]{1,0:T(8,128)(2,1)S(1)} %get-tuple-element.38), channel_id=1, source_target_pairs={{0,2},{2,4},{4,6},{6,8},{8,10},{10,12},{12,14},{14,16},{16,18},{18... | collective-permute-start | bytes 98312 | tf_op jit(solution)/shard_map/ppermute | solution.py:22
  62.5 7.9 %collective-permute-start.13 = (bf16[64,256]{1,0:T(8,128)(2,1)S(1)}, bf16[64,256]{1,0:T(8,128)(2,1)S(1)}, u32[]{:S(2)}, u32[]{:S(2)}) collective-permute-start(bf16[64,256]{1,0:T(8,128)(2,1)S(1)} %get-tuple-element.39), channel_id=1, source_target_pairs={{0,254},{2,0},{4,2},{6,4},{8,6},{10,8},{12,10},{14,12},{16,14},{18... | collective-permute-start | bytes 98312 | tf_op jit(solution)/shard_map/ppermute | solution.py:22
  73.7 2.5 %collective-permute-start.14 = (bf16[512,256]{1,0:T(8,128)(2,1)S(1)}, bf16[512,256]{1,0:T(8,128)(2,1)S(1)}, u32[]{:S(2)}, u32[]{:S(2)}) collective-permute-start(bf16[512,256]{1,0:T(8,128)(2,1)S(1)} %layer_messages_1.1.sum_own), channel_id=1, source_target_pairs={{0,1},{1,0},{2,3},{3,2},{4,5},{5,4},{6,7},{7,6},{8,9},{9,8},{10,11... | collective-permute-start | bytes 786440 | tf_op jit(solution)/shard_map/ppermute | solution.py:26
  78.9 26.0 %collective-permute-start.17 = (bf16[512,256]{1,0:T(8,128)(2,1)S(1)}, bf16[512,256]{1,0:T(8,128)(2,1)S(1)}, u32[]{:S(2)}, u32[]{:S(2)}) collective-permute-start(bf16[512,256]{1,0:T(8,128)(2,1)S(1)} %get-tuple-element.42.refs_0_), channel_id=1, source_target_pairs={{0,254},{2,0},{4,2},{6,4},{8,6},{10,8},{12,10},{14,12},{16,14},{18... | collective-permute-start | bytes 786440 | tf_op jit(solution)/shard_map/ppermute | solution.py:22
  86.1 18.9 %collective-permute-start.18 = (bf16[512,256]{1,0:T(8,128)(2,1)S(1)}, bf16[512,256]{1,0:T(8,128)(2,1)}, u32[]{:S(2)}, u32[]{:S(2)}) collective-permute-start(bf16[512,256]{1,0:T(8,128)(2,1)S(1)} %get-tuple-element.42.refs_0_), channel_id=1, source_target_pairs={{0,2},{2,4},{4,6},{6,8},{8,10},{10,12},{12,14},{14,16},{16,18},{18... | collective-permute-start | bytes 786440 | tf_op jit(solution)/shard_map/ppermute | solution.py:22
  90.0 19.2 %collective-permute-start.15 = (bf16[512,256]{1,0:T(8,128)(2,1)S(1)}, bf16[512,256]{1,0:T(8,128)(2,1)S(1)}, u32[]{:S(2)}, u32[]{:S(2)}) collective-permute-start(bf16[512,256]{1,0:T(8,128)(2,1)S(1)} %get-tuple-element.42.refs_0_), channel_id=1, source_target_pairs={{0,252},{2,254},{4,0},{6,2},{8,4},{10,6},{12,8},{14,10},{16,12},{1... | collective-permute-start | bytes 786440 | tf_op jit(solution)/shard_map/ppermute | solution.py:22
  103.2 12.3 %collective-permute-start.16 = (bf16[512,256]{1,0:T(8,128)(2,1)S(1)}, bf16[512,256]{1,0:T(8,128)(2,1)S(1)}, u32[]{:S(2)}, u32[]{:S(2)}) collective-permute-start(bf16[512,256]{1,0:T(8,128)(2,1)S(1)} %get-tuple-element.42.refs_0_), channel_id=1, source_target_pairs={{0,4},{2,6},{4,8},{6,10},{8,12},{10,14},{12,16},{14,18},{16,20},{1... | collective-permute-start | bytes 786440 | tf_op jit(solution)/shard_map/ppermute | solution.py:22
  118.7 3.8 %collective-permute-start.19 = (bf16[1024,256]{1,0:T(8,128)(2,1)S(1)}, bf16[1024,256]{1,0:T(8,128)(2,1)S(1)}, u32[]{:S(2)}, u32[]{:S(2)}) collective-permute-start(bf16[1024,256]{1,0:T(8,128)(2,1)S(1)} %decode_far.1.sum_own), channel_id=1, source_target_pairs={{0,1},{1,0},{2,3},{3,2},{4,5},{5,4},{6,7},{7,6},{8,9},{9,8},{10,11... | collective-permute-start | bytes 1572872 | tf_op jit(solution)/shard_map/ppermute | solution.py:26
  (24 other events, 165.9 us)

commit v2 on v0

v2 whole, which is shorter than its diff:
```python
import functools

import jax
import jax.numpy as jnp
from jax import lax
from jax.experimental import pallas as pl
from jax.experimental.pallas import tpu as pltpu
from jax.sharding import PartitionSpec as P

REACH = 2
LAYERS = 2
MARGIN = 64
HALF = 256
LANES = 128
F32 = jnp.float32
BF16 = jnp.bfloat16
I32 = jnp.int32
VMEM_LIMIT = 36 * 1024 * 1024


def swap(value):
    return lax.ppermute(value, "feat", [(0, 1), (1, 0)])


def flat(partners):
    return [(2 * s + c, 2 * t + e) for (s, c), (t, e) in partners.items()]


def far_pairs(count):
    partners = {}
    for s in range(count):
        near = s + 1 if s % 2 else s - 1
        partners[s, 0] = (near % count, 0)
        skip = s + 2 if s % 4 >= 2 else s - 2
        partners[s, 1] = (skip if 0 <= skip < count else s ^ 1, 1)
    return flat(partners)


def line_pairs(count):
    partners = {}
    for s in range(count):
        partners[s, 0] = (s ^ 1, 0)
        partners[s, 1] = (s ^ 2, 1)
    return flat(partners)


def halo_pairs(count):
    partners = {}
    for s in range(count):
        partners[s, 1] = ((s + 1) % count, 0)
        partners[(s + 1) % count, 0] = (s, 1)
    return flat(partners)


def exchange(value, pairs):
    return lax.ppermute(value, ("band", "feat"), pairs(lax.axis_size("band")))


def silu(v):
    half = 0.5 * v
    return half + half * jnp.tanh(half)


def dot(a, b):
    return jnp.dot(a, b, preferred_element_type=F32)


def window(index, size=HALF):
    return pl.ds(pl.multiple_of(index * size, size), size)


def far_sent(meta):
    return (1 - meta[0]) * (1 + 2 * meta[2]) + meta[0] * 4 * meta[3]


def line_sent(meta):
    return (1 - meta[0]) * (3 - 2 * meta[2]) + meta[0] * (4 - 4 * meta[3])


far_received = line_sent
line_received = far_sent


def column(row):
    parts = [
        jnp.broadcast_to(row[:, start : start + LANES], (LANES, LANES)).T
        for start in range(0, row.shape[1], LANES)
    ]
    return parts[0] if len(parts) == 1 else jnp.concatenate(parts, axis=0)


def hot_columns(col, width):
    ids = lax.broadcasted_iota(I32, col.shape, 1)
    parts = [
        jnp.where(col == ids + start, 1.0, 0.0).astype(BF16) for start in range(0, width, LANES)
    ]
    return parts[0] if len(parts) == 1 else jnp.concatenate(parts, axis=1)


def hot_rows(row, height):
    ids = lax.broadcasted_iota(I32, (height, row.shape[1]), 0)
    return jnp.where(row == ids, 1.0, 0.0).astype(BF16)


def call(kernel, name, operands, specs, outs, flops, scratch=()):
    size = sum(x.size * x.dtype.itemsize for x in outs)
    return pl.pallas_call(
        kernel,
        name=name,
        grid=(1,),
        in_specs=specs,
        out_specs=[whole(x) for x in outs],
        out_shape=list(outs),
        scratch_shapes=list(scratch),
        compiler_params=pltpu.CompilerParams(vmem_limit_bytes=VMEM_LIMIT),
        cost_estimate=pl.CostEstimate(flops=flops, bytes_accessed=2 * size, transcendentals=0),
    )(*operands)


def whole(x):
    return pl.BlockSpec(x.shape, lambda i, n=len(x.shape): (0,) * n)


def part(x, *index):
    lead = len(index)
    rest = x.shape[lead:]
    return pl.BlockSpec((None,) * lead + rest, lambda i, where=index + (0,) * len(rest): where)


SMEM = pl.BlockSpec(memory_space=pltpu.SMEM)


def shape(*dims, dtype=BF16):
    return jax.ShapeDtypeStruct(dims, dtype)


def encode_begin_kernel(meta, own, w_own, out):
    for start in range(0, own.shape[0], HALF):
        rows = pl.ds(start, HALF)
        out[rows, :] = dot(own[rows, :], w_own[window(meta[0]), :])


def gather_slots(senders_row, sent, out):
    for start in range(0, senders_row.shape[1], HALF):
        col = column(senders_row[:, start : start + HALF])
        out[pl.ds(start, HALF), :] = dot(hot_columns(col, sent.shape[0]), sent[...]).astype(BF16)


def encode_far_kernel(meta, own, other, begun, w_own, w_other, senders, sent, piece):
    mine, rest = window(meta[0]), window(1 - meta[0])
    for start in range(0, own.shape[0], HALF):
        rows = pl.ds(start, HALF)
        a, b = own[rows, :], other[rows, :]
        sent[rows, mine] = (begun[rows, :] + dot(b, w_own[rest, :])).astype(BF16)
        sent[rows, rest] = (dot(a, w_other[mine, :]) + dot(b, w_other[rest, :])).astype(BF16)
    gather_slots(senders[pl.ds(far_sent(meta), 1), :], sent, piece)


def encode_line_kernel(meta, sent, senders, piece):
    gather_slots(senders[pl.ds(line_sent(meta), 1), :], sent, piece)


def scatter(row, message, total_in, nodes, put):
    for index in range(nodes // HALF):
        value = dot(hot_rows(row - index * HALF, HALF), message[...])
        if total_in is not None:
            value = value + total_in[pl.ds(index * HALF, HALF), :]
        put(index, value)


def live_targets(targets, live, offset, columns=slice(None)):
    pick = pl.ds(offset, 1)
    return jnp.where(live[pick, columns] > 0, targets[pick, columns], -1)


def encode_prepare_kernel(
    meta, own, other, w1, w1_other, w2, w2_other, sent, senders, targets, live,
    total, before_line, before_far, self_term, recv, message,
):
    mine, rest = window(meta[0]), window(1 - meta[0])
    nodes = own.shape[0]
    for start in range(0, nodes, HALF):
        rows = pl.ds(start, HALF)
        a, b = own[rows, :], other[rows, :]
        recv[rows, mine] = (dot(a, w1[mine, :]) + dot(b, w1[rest, :])).astype(BF16)
        recv[rows, rest] = (dot(a, w1_other[mine, :]) + dot(b, w1_other[rest, :])).astype(BF16)
    a, b = own[mine, :], other[mine, :]
    self_term[:, mine] = dot(a, w2[mine, :]) + dot(b, w2[rest, :])
    self_term[:, rest] = dot(a, w2_other[mine, :]) + dot(b, w2_other[rest, :])
    gather_slots(targets[pl.ds(line_received(meta), 1), :], recv, before_line)
    gather_slots(targets[pl.ds(far_received(meta), 1), :], recv, before_far)
    pick = pl.ds(REACH, 1)
    from_rows = hot_columns(column(senders[pick, mine]), sent.shape[0])
    to_rows = hot_columns(column(targets[pick, mine]), nodes)
    message[...] = silu(dot(from_rows, sent[...]) + dot(to_rows, recv[...])).astype(BF16)

    def put(index, value):
        total[pl.ds(index * HALF, HALF), :] = value

    scatter(live_targets(targets, live, REACH, mine), message, None, nodes, put)


def encode_line_sum_kernel(meta, rows, before, targets, live, total, out, message):
    message[...] = silu(rows[...].astype(F32) + before[...].astype(F32)).astype(BF16)

    def put(index, value):
        out[pl.ds(index * HALF, HALF), :] = value

    row = live_targets(targets, live, line_received(meta))
    scatter(row, message, total, total.shape[0], put)


def encode_far_sum_kernel(meta, rows, before, targets, live, total, out_own, out_other, message):
    message[...] = silu(rows[...].astype(F32) + before[...].astype(F32)).astype(BF16)
    row = live_targets(targets, live, far_received(meta))
    for out, half in ((out_other, 1 - meta[0]), (out_own, meta[0])):
        value = dot(hot_rows(row - half * HALF, HALF), message[...]) + total[window(half), :]
        out[...] = value.astype(out.dtype)


def put_edge(meta, now, w0, w0_other, edge):
    mine, rest = window(meta[0]), window(1 - meta[0])
    rows = now[pl.ds(pl.multiple_of(meta[0] * (HALF - MARGIN), MARGIN), MARGIN), :]
    edge[:, mine] = dot(rows, w0[...]).astype(BF16)
    edge[:, rest] = dot(rows, w0_other[...]).astype(BF16)


def encode_update_kernel(
    meta, own, other, self_term, sum_own, sum_other, w3, w3_other, w0, w0_other, now, edge
):
    mine, rest = window(meta[0]), window(1 - meta[0])
    summed = (sum_own[...] + sum_other[...].astype(F32)).astype(BF16)
    for cols, latent, w in ((mine, own, w3), (rest, other, w3_other)):
        step = silu(self_term[:, cols] + dot(summed, w[...]))
        now[:, cols] = (latent[mine, :].astype(F32) + step).astype(BF16)
    put_edge(meta, now, w0, w0_other, edge)


def layer_project_kernel(
    last, meta, own, other, w0, w0_other, w1, w1_other, w2, w2_other,
    sent_own, sent_other, recv, self_own, *self_other,
):
    mine, rest = window(meta[0]), window(1 - meta[0])
    for cols, w in ((mine, w0), (rest, w0_other)):
        sent_own[:, cols] = dot(own[...], w[...]).astype(BF16)
        sent_other[:, cols] = dot(other[...], w[...]).astype(BF16)
    for cols, w in ((mine, w1), (rest, w1_other)):
        recv[:, cols] = dot(own[...], w[...])
    for cols, w in ((mine, w2), (rest, w2_other)):
        self_own[:, cols] = dot(own[...], w[...])
        if last:
            self_other[0][:, cols] = dot(other[...], w[...])


def layer_gather_kernel(meta, own, other, senders, out):
    mine = window(meta[0])
    base = meta[1] * (2 * HALF)
    for k in range(senders.shape[0]):
        local = senders[k : k + 1, mine] - base
        col = column(local - meta[0] * HALF)
        col_other = column(local - (1 - meta[0]) * HALF)
        value = dot(hot_columns(col, HALF), own[...])
        value = value + dot(hot_columns(col_other, HALF), other[...])
        out[k] = value.astype(BF16)


def layer_sum(meta, gathered, recv, near, far, senders, live, halo, total):
    mine = window(meta[0])
    nodes = 2 * HALF
    base = meta[1] * nodes
    halo[pl.ds(pl.multiple_of(meta[0] * MARGIN, MARGIN), MARGIN), :] = near[...]
    halo[pl.ds(pl.multiple_of((1 - meta[0]) * MARGIN, MARGIN), MARGIN), :] = far[...]
    count = senders.shape[0]
    for k in range(count):
        local = senders[k : k + 1, mine] - base
        where = jnp.where(local < 0, local + MARGIN, local - nodes + MARGIN)
        where = jnp.where((local >= 0) & (local < nodes), -1, where)
        flags = column(live[k : k + 1, mine]).astype(F32)
        flags = jnp.concatenate([flags] * (recv.shape[1] // LANES), axis=1)
        pre = dot(hot_columns(column(where), 2 * MARGIN), halo[...])
        pre = pre + gathered[k].astype(F32) + recv[...]
        message = (silu(pre) * flags).astype(BF16).astype(F32)
        total[...] = message if k == 0 else total[...] + message
    return total[...].astype(BF16)


def layer_update_kernel(
    meta, gathered, recv, near, far, senders, live, now, self_term, w3, w3_other, w0, w0_other,
    out, edge, halo, total,
):
    mine, rest = window(meta[0]), window(1 - meta[0])
    summed = layer_sum(meta, gathered, recv, near, far, senders, live, halo, total)
    for cols, w in ((mine, w3), (rest, w3_other)):
        step = silu(self_term[:, cols] + dot(summed, w[...]))
        out[:, cols] = (now[:, cols].astype(F32) + step).astype(BF16)
    put_edge(meta, out, w0, w0_other, edge)


def layer_sum_kernel(meta, gathered, recv, near, far, senders, live, out, halo, total):
    out[...] = layer_sum(meta, gathered, recv, near, far, senders, live, halo, total)


def last_update_kernel(
    meta, now_own, now_other, self_own, self_other, sum_own, sum_other, w3, w3_other,
    w0, w0_other, out, sent, now,
):
    mine, rest = window(meta[0]), window(1 - meta[0])
    for rows, latent, self_term, summed in (
        (mine, now_own, self_own, sum_own),
        (rest, now_other, self_other, sum_other),
    ):
        for cols, w in ((mine, w3), (rest, w3_other)):
            step = silu(self_term[:, cols] + dot(summed[...], w[...]))
            now[:, cols] = (latent[:, cols].astype(F32) + step).astype(BF16)
        out[rows, :] = now[:, mine]
        for cols, w in ((mine, w0), (rest, w0_other)):
            sent[rows, cols] = dot(now[...], w[...]).astype(BF16)


def decode_prepare_kernel(
    meta, own, other, w1, w1_other, w2, targets,
    before_own, before_line, before_far, self_term, recv,
):
    mine, rest = window(meta[0]), window(1 - meta[0])
    for start in range(0, own.shape[0], HALF):
        rows = pl.ds(start, HALF)
        a, b = own[rows, :], other[rows, :]
        recv[rows, mine] = (dot(a, w1[mine, :]) + dot(b, w1[rest, :])).astype(BF16)
        recv[rows, rest] = (dot(a, w1_other[mine, :]) + dot(b, w1_other[rest, :])).astype(BF16)
        self_term[rows, :] = dot(a, w2[mine, :]) + dot(b, w2[rest, :])
    half = before_own.shape[0]
    gather_slots(targets[pl.ds(REACH, 1), window(meta[0], half)], recv, before_own)
    gather_slots(targets[pl.ds(line_received(meta), 1), :], recv, before_line)
    gather_slots(targets[pl.ds(far_received(meta), 1), :], recv, before_far)


def decode_sum_kernel(kind, meta, sent, before, senders, targets, live, *refs):
    total, out, message = refs if kind != "own" else (None,) + refs
    slots = before.shape[0]
    if kind == "own":
        offset, columns = REACH, window(meta[0], slots)
    else:
        offset = (line_received if kind == "line" else far_received)(meta)
        columns = slice(None)
    from_row = senders[pl.ds(offset, 1), columns]
    for start in range(0, slots, HALF):
        rows = pl.ds(start, HALF)
        hot = hot_columns(column(from_row[:, start : start + HALF]), sent.shape[0])
        pre = dot(hot, sent[...]) + before[rows, :].astype(F32)
        message[rows, :] = silu(pre).astype(BF16)

    def put(index, value):
        out[pl.ds(index * HALF, HALF), :] = value.astype(out.dtype)

    scatter(live_targets(targets, live, offset, columns), message, total, out.shape[0], put)


def final_kernel(meta, own, self_term, sum_own, sum_other, w3, out):
    for start in range(0, own.shape[0], HALF):
        rows = pl.ds(start, HALF)
        summed = (sum_own[rows, :].astype(F32) + sum_other[rows, :].astype(F32)).astype(BF16)
        step = silu(self_term[rows, :] + dot(summed, w3[...]))
        out[rows, :] = (own[rows, :].astype(F32) + step).astype(BF16)


def body(
    grid_latent,
    mesh_latent,
    encode_weights,
    layer_weights,
    decode_weights,
    encode_senders,
    encode_targets,
    encode_live,
    mesh_senders,
    mesh_live,
    decode_senders,
    decode_targets,
    decode_live,
):
    band = lax.axis_index("band")
    meta = jnp.stack([lax.axis_index("feat"), band, band % 2, band // 2 % 2]).astype(I32)
    grid_rows, cols = grid_latent.shape
    mesh_rows = mesh_latent.shape[0]
    full = 2 * cols
    senders, targets, live = encode_senders[0], encode_targets[0], encode_live[0]
    slots = senders.shape[1]

    grid_other = swap(grid_latent)
    first_other = swap(encode_weights[0])
    (begun,) = call(
        encode_begin_kernel,
        "encode_begin",
        (meta, grid_latent, encode_weights),
        [SMEM, whole(grid_latent), part(encode_weights, 0)],
        [shape(grid_rows, cols, dtype=F32)],
        2 * grid_rows * cols * cols,
    )
    operands = (meta, grid_latent, grid_other, begun, encode_weights, first_other, senders)
    sent, far_piece = call(
        encode_far_kernel,
        "encode_far",
        operands,
        [SMEM] + [whole(x) for x in operands[1:4]]
        + [part(encode_weights, 0), whole(first_other), whole(senders)],
        [shape(grid_rows, full), shape(slots, full)],
        2 * full * (grid_rows * full + slots * grid_rows),
    )
    far_rows = exchange(far_piece, far_pairs)
    operands = (meta, sent, senders)
    (line_piece,) = call(
        encode_line_kernel,
        "encode_line",
        operands,
        [SMEM, whole(sent), whole(senders)],
        [shape(slots, full)],
        2 * full * slots * grid_rows,
    )
    line_rows = exchange(line_piece, line_pairs)

    mesh_source, encode_source, layer_source, decode_source, _ = lax.optimization_barrier(
        (mesh_latent, encode_weights, layer_weights, decode_weights, sent)
    )
    mesh_other = swap(mesh_source)
    encode_other = swap(encode_source)
    layer_other = swap(layer_source)
    decode_other = swap(decode_source)

    operands = (
        meta, mesh_latent, mesh_other, encode_weights, encode_other, encode_weights, encode_other,
        sent, senders, targets, live,
    )
    total, before_line, before_far, self_term = call(
        encode_prepare_kernel,
        "encode_prepare",
        operands,
        [SMEM, whole(mesh_latent), whole(mesh_other)]
        + [part(operands[3 + i], 1 + i // 2) for i in range(4)]
        + [whole(x) for x in operands[7:]],
        [
            shape(mesh_rows, full, dtype=F32),
            shape(slots, full),
            shape(slots, full),
            shape(HALF, full, dtype=F32),
        ],
        2 * full * mesh_rows * (full + 3 * slots),
        [pltpu.VMEM((mesh_rows, full), BF16), pltpu.VMEM((HALF, full), BF16)],
    )
    operands = (meta, line_rows, before_line, targets, live, total)
    (total,) = call(
        encode_line_sum_kernel,
        "encode_line_sum",
        operands,
        [SMEM] + [whole(x) for x in operands[1:]],
        [shape(mesh_rows, full, dtype=F32)],
        2 * full * mesh_rows * slots,
        [pltpu.VMEM((slots, full), BF16)],
    )
    operands = (meta, far_rows, before_far, targets, live, total)
    sum_own, sum_other = call(
        encode_far_sum_kernel,
        "encode_far_sum",
        operands,
        [SMEM] + [whole(x) for x in operands[1:]],
        [shape(HALF, full, dtype=F32), shape(HALF, full)],
        2 * full * mesh_rows * slots,
        [pltpu.VMEM((slots, full), BF16)],
    )
    operands = (
        meta, mesh_latent, mesh_other, self_term, sum_own, swap(sum_other),
        encode_weights, encode_other, layer_weights, layer_other,
    )
    now, edge = call(
        encode_update_kernel,
        "encode_update",
        operands,
        [SMEM] + [whole(x) for x in operands[1:6]]
        + [part(encode_weights, 3), part(encode_other, 3)]
        + [part(layer_weights, 0, 0), part(layer_other, 0, 0)],
        [shape(HALF, full), shape(MARGIN, full)],
        2 * HALF * full * full,
    )

    senders_t, live_t = mesh_senders.T, mesh_live.T
    degree = senders_t.shape[0]
    for layer in range(LAYERS):
        last = layer == LAYERS - 1
        near = exchange(edge, halo_pairs)
        now_other = swap(now)
        operands = (meta, now, now_other) + (layer_weights, layer_other) * 3
        results = call(
            functools.partial(layer_project_kernel, last),
            f"layer_project_{layer}",
            operands,
            [SMEM, whole(now), whole(now_other)]
            + [part(operands[3 + i], layer, i // 2) for i in range(6)],
            [shape(HALF, full)] * 2 + [shape(HALF, full, dtype=F32)] * (3 if last else 2),
            2 * HALF * full * full * 4,
        )
        sent_own, sent_other, recv, self_own = results[:4]
        operands = (meta, sent_own, sent_other, senders_t)
        (gathered,) = call(
            layer_gather_kernel,
            f"layer_gather_{layer}",
            operands,
            [SMEM] + [whole(x) for x in operands[1:]],
            [shape(degree, HALF, full)],
            2 * degree * HALF * full * mesh_rows,
        )
        operands = (meta, gathered, recv, near, swap(near), senders_t, live_t)
        scratch = [pltpu.VMEM((2 * MARGIN, full), BF16), pltpu.VMEM((HALF, full), F32)]
        if last:
            (summed,) = call(
                layer_sum_kernel,
                f"layer_sum_{layer}",
                operands,
                [SMEM] + [whole(x) for x in operands[1:]],
                [shape(HALF, full)],
                2 * degree * HALF * full * 2 * MARGIN,
                scratch,
            )
            continue
        operands += (now, self_own) + (layer_weights, layer_other) * 2
        now, edge = call(
            layer_update_kernel,
            f"layer_update_{layer}",
            operands,
            [SMEM] + [whole(x) for x in operands[1:9]]
            + [part(layer_weights, layer, 3), part(layer_other, layer, 3)]
            + [part(layer_weights, layer + 1, 0), part(layer_other, layer + 1, 0)],
            [shape(HALF, full), shape(MARGIN, full)],
            2 * HALF * full * (degree * 2 * MARGIN + full),
            scratch,
        )
    operands = (
        meta, now, now_other, self_own, results[4], summed, swap(summed),
        layer_weights, layer_other, decode_weights, decode_other,
    )
    mesh_now, sent = call(
        last_update_kernel,
        "last_update",
        operands,
        [SMEM] + [whole(x) for x in operands[1:7]]
        + [part(layer_weights, LAYERS - 1, 3), part(layer_other, LAYERS - 1, 3)]
        + [part(decode_weights, 0), part(decode_other, 0)],
        [shape(mesh_rows, cols), shape(mesh_rows, full)],
        2 * mesh_rows * full * full * 2,
        [pltpu.VMEM((HALF, full), BF16)],
    )

    far_rows = exchange(sent, far_pairs)
    line_rows = exchange(sent, line_pairs)
    senders, targets, live = decode_senders[0], decode_targets[0], decode_live[0]
    slots = senders.shape[1]
    operands = (
        meta, grid_latent, grid_other, decode_weights, decode_other, decode_weights, targets
    )
    before_own, before_line, before_far, self_term = call(
        decode_prepare_kernel,
        "decode_prepare",
        operands,
        [SMEM, whole(grid_latent), whole(grid_other)]
        + [part(decode_weights, 1), part(decode_other, 1), part(decode_weights, 2), whole(targets)],
        [
            shape(slots // 2, full),
            shape(slots, full),
            shape(slots, full),
            shape(grid_rows, cols, dtype=F32),
        ],
        2 * full * grid_rows * (full + 5 * slots // 2),
        [pltpu.VMEM((grid_rows, full), BF16)],
    )
    total = None
    for kind, rows, before in (
        ("own", sent, before_own),
        ("line", line_rows, before_line),
        ("far", far_rows, before_far),
    ):
        operands = (meta, rows, before, senders, targets, live)
        if total is not None:
            operands += (total,)
        (total,) = call(
            functools.partial(decode_sum_kernel, kind),
            f"decode_{kind}",
            operands,
            [SMEM] + [whole(x) for x in operands[1:]],
            [shape(grid_rows, full, dtype=BF16 if kind == "far" else F32)],
            2 * full * before.shape[0] * (grid_rows + mesh_rows),
            [pltpu.VMEM(before.shape, BF16)],
        )
    operands = (meta, grid_latent, self_term, total, swap(total), decode_weights)
    (grid_now,) = call(
        final_kernel,
        "final_update",
        operands,
        [SMEM] + [whole(x) for x in operands[1:5]] + [part(decode_weights, 3)],
        [shape(grid_rows, cols)],
        2 * full * grid_rows * cols,
    )
    return mesh_now, grid_now


def solution(mesh):
    placed = (
        P("band", "feat"),
        P("band", "feat"),
        P(None, None, "feat"),
        P(None, None, None, "feat"),
        P(None, None, "feat"),
        P("band", None, None),
        P("band", None, None),
        P("band", None, None),
        P("band", None),
        P("band", None),
        P("band", None, None),
        P("band", None, None),
        P("band", None, None),
    )
    return jax.shard_map(
        body,
        mesh=mesh,
        in_specs=placed,
        out_specs=(P("band", "feat"), P("band", "feat")),
        check_vma=False,
    )
```

time: 321 us -> 111 us (0.35)
  the two profiles are of different devices: /device:TPU:129 before, /device:TPU:1 now
where the time goes in v2:
time: 111 us; the launch traced here: 110 us
  Pallas kernels  40.4 us (36%)
  waiting for transfers between devices  37.7 us (34%)
  starting transfers between devices  28.4 us (26%)
  local copies, waits for them, and re-layouts  2.8 us (3%)
    pallas_call x19, Pallas kernels, call(): pl.pallas_call(kernel, name=name, grid=(1,), in_specs=specs, out_specs=[w...  40.4 us
    ppermute x6, waiting for transfers between devices, exchange(): return lax.ppermute(value, ('band', 'feat'), pairs(lax.axis_size('band')))  30.9 us
    ppermute x13, starting transfers between devices, swap(): return lax.ppermute(value, 'feat', [(0, 1), (1, 0)])  26.6 us
    ppermute x13, waiting for transfers between devices, swap(): return lax.ppermute(value, 'feat', [(0, 1), (1, 0)])  6.83 us
  transfers between devices with their start and end apart: 19, of which 10 were waited for; matrix products, arithmetic and copies ran while one was open for 2% of the time, Pallas kernels for 27%

profile of v2, /device:TPU:1, one launch (start us, length us, event | category | flops | bytes accessed | tf_op | source)
XLA Modules:
  0.0 110.4 jit_solution(9786866687083945314)
XLA Ops:
  0.6 3.3 %collective-permute-start = (bf16[1024,256]{1,0:T(8,128)(2,1)}, bf16[1024,256]{1,0:T(8,128)(2,1)S(1)}, u32[]{:S(2)}, u32[]{:S(2)}) collective-permute-start(bf16[1024,256]{1,0:T(8,128)(2,1)} %own.11), channel_id=1, source_target_pairs={{0,1},{1,0},{2,3},{3,2},{4,5},{5,4},{6,7},{7,6},{8,9},{9,8},{10,11... | collective-permute-start | bytes 1572872 | tf_op jit(solution)/shard_map/ppermute | solution.py:22
  8.2 2.5 %encode_far.1 = (bf16[1024,512]{1,0:T(8,128)(2,1)S(1)}, bf16[512,512]{1,0:T(8,128)(2,1)S(1)}) custom-call(s32[4]{0:T(128)S(1)} %pad_add_fusion.meta, bf16[1024,256]{1,0:T(8,128)(2,1)S(1)} %copy-done.2, bf16[1024,256]{1,0:T(8,128)(2,1)S(1)} %collective-permute-done.other, f32[1024,256]{1,0:T(8,128)S(1)} %encode_begin.1.begun, bf16[4,512,256]{2,1,0:T(8,128)(2,1)} %w3.4, ...), custom_call_target="tpu_custom_call" | custom-call | flops 1073741824 | bytes 3145728 | tf_op jit(solution)/shard_map/encode_far/pallas_call | solution.py:107
  14.1 8.7 %collective-permute-start.2 = (bf16[512,256]{1,0:T(8,128)(2,1)S(1)}, bf16[512,256]{1,0:T(8,128)(2,1)S(1)}, u32[]{:S(2)}, u32[]{:S(2)}) collective-permute-start(bf16[512,256]{1,0:T(8,128)(2,1)S(1)} %copy-done.4), channel_id=1, source_target_pairs={{0,1},{1,0},{2,3},{3,2},{4,5},{5,4},{6,7},{7,6},{8,9},{9,8},{10,11... | collective-permute-start | bytes 786440 | tf_op jit(solution)/shard_map/ppermute | solution.py:22
  24.0 3.0 %encode_prepare.1 = (f32[512,512]{1,0:T(8,128)S(1)}, bf16[512,512]{1,0:T(8,128)(2,1)S(1)}, bf16[512,512]{1,0:T(8,128)(2,1)S(1)}, f32[256,512]{1,0:T(8,128)S(1)}) custom-call(s32[4]{0:T(128)S(1)} %pad_add_fusion.meta, bf16[512,256]{1,0:T(8,128)(2,1)S(1)} %copy-done.4, bf16[512,256]{1,0:T(8,128)(2,1)S(1)} %collective-permute-done.2.other, ...), custom_call_target="tpu_custom_call" | custom-call | flops 1073741824 | bytes 5242880 | tf_op jit(solution)/shard_map/encode_prepare/pallas_call | solution.py:107
  26.9 3.8 %collective-permute-done.5.rows = bf16[512,512]{1,0:T(8,128)(2,1)S(1)} collective-permute-done((bf16[512,512]{1,0:T(8,128)(2,1)S(1)}, bf16[512,512]{1,0:T(8,128)(2,1)S(1)}, u32[]{:S(2)}, u32[]{:S(2)}) %collective-permute-start.5) | collective-permute-done | bytes 524320 | tf_op jit(solution)/shard_map/ppermute | solution.py:56
  31.9 8.6 %collective-permute-done.4.rows = bf16[512,512]{1,0:T(8,128)(2,1)S(1)} collective-permute-done((bf16[512,512]{1,0:T(8,128)(2,1)S(1)}, bf16[512,512]{1,0:T(8,128)(2,1)S(1)}, u32[]{:S(2)}, u32[]{:S(2)}) %collective-permute-start.4) | collective-permute-done | bytes 524320 | tf_op jit(solution)/shard_map/ppermute | solution.py:56
  43.3 1.6 %encode_update.1 = (bf16[256,512]{1,0:T(8,128)(2,1)S(1)}, bf16[64,512]{1,0:T(8,128)(2,1)S(1)}) custom-call(s32[4]{0:T(128)S(1)} %pad_add_fusion.meta, bf16[512,256]{1,0:T(8,128)(2,1)S(1)} %copy-done.4, bf16[512,256]{1,0:T(8,128)(2,1)S(1)} %collective-permute-done.2.other, f32[256,512]{1,0:T(8,128)S(1)} %get-tuple-element.36.self_term, ...), custom_call_target="tpu_custom_call" | custom-call | flops 134217728 | bytes 655360 | tf_op jit(solution)/shard_map/encode_update/pallas_call | solution.py:107
  45.6 3.7 %collective-permute-done.9.near = bf16[64,512]{1,0:T(8,128)(2,1)S(1)} collective-permute-done((bf16[64,512]{1,0:T(8,128)(2,1)S(1)}, bf16[64,512]{1,0:T(8,128)(2,1)S(1)}, u32[]{:S(2)}, u32[]{:S(2)}) %collective-permute-start.9) | collective-permute-done | bytes 65568 | tf_op jit(solution)/shard_map/ppermute | solution.py:56
  49.3 7.0 %collective-permute-start.10 = (bf16[64,512]{1,0:T(8,128)(2,1)S(1)}, bf16[64,512]{1,0:T(8,128)(2,1)S(1)}, u32[]{:S(2)}, u32[]{:S(2)}) collective-permute-start(bf16[64,512]{1,0:T(8,128)(2,1)S(1)} %collective-permute-done.9.near), channel_id=1, source_target_pairs={{0,1},{1,0},{2,3},{3,2},{4,5},{5,4},{6,7},{7,6},{8,9},{9,8},{10,11... | collective-permute-start | bytes 196616 | tf_op jit(solution)/shard_map/ppermute | solution.py:22
  57.6 1.8 %layer_gather_0.1.gathered = bf16[8,256,512]{2,1,0:T(8,128)(2,1)S(1)} custom-call(s32[4]{0:T(128)S(1)} %pad_add_fusion.meta, bf16[256,512]{1,0:T(8,128)(2,1)S(1)} %get-tuple-element.45.own, bf16[256,512]{1,0:T(8,128)(2,1)S(1)} %get-tuple-element.46.other, s32[8,512]{1,0:T(8,128)S(1)} %bitcast.26), custom_call_target="tpu_custom_call" | custom-call | flops 1073741824 | bytes 4194304 | tf_op jit(solution)/shard_map/layer_gather_0/pallas_call | solution.py:107
  59.5 3.2 %layer_update_0.1 = (bf16[256,512]{1,0:T(8,128)(2,1)S(1)}, bf16[64,512]{1,0:T(8,128)(2,1)S(1)}) custom-call(s32[4]{0:T(128)S(1)} %pad_add_fusion.meta, bf16[8,256,512]{2,1,0:T(8,128)(2,1)S(1)} %layer_gather_0.1.gathered, f32[256,512]{1,0:T(8,128)S(1)} %get-tuple-element.47.recv, bf16[64,512]{1,0:T(8,128)(2,1)S(1)} %collective-permute-done.9.near, ...), custom_call_target="tpu_custom_call" | custom-call | flops 402653184 | bytes 655360 | tf_op jit(solution)/shard_map/layer_update_0/pallas_call | solution.py:107
  62.9 3.7 %collective-permute-done.12.near = bf16[64,512]{1,0:T(8,128)(2,1)S(1)} collective-permute-done((bf16[64,512]{1,0:T(8,128)(2,1)S(1)}, bf16[64,512]{1,0:T(8,128)(2,1)S(1)}, u32[]{:S(2)}, u32[]{:S(2)}) %collective-permute-start.12) | collective-permute-done | bytes 65568 | tf_op jit(solution)/shard_map/ppermute | solution.py:56
  66.6 5.8 %collective-permute-start.13 = (bf16[64,512]{1,0:T(8,128)(2,1)S(1)}, bf16[64,512]{1,0:T(8,128)(2,1)S(1)}, u32[]{:S(2)}, u32[]{:S(2)}) collective-permute-start(bf16[64,512]{1,0:T(8,128)(2,1)S(1)} %collective-permute-done.12.near), channel_id=1, source_target_pairs={{0,1},{1,0},{2,3},{3,2},{4,5},{5,4},{6,7},{7,6},{8,9},{9,8},{10,11... | collective-permute-start | bytes 196616 | tf_op jit(solution)/shard_map/ppermute | solution.py:22
  73.8 1.9 %layer_gather_1.1.gathered = bf16[8,256,512]{2,1,0:T(8,128)(2,1)S(1)} custom-call(s32[4]{0:T(128)S(1)} %pad_add_fusion.meta, bf16[256,512]{1,0:T(8,128)(2,1)S(1)} %get-tuple-element.53.own, bf16[256,512]{1,0:T(8,128)(2,1)S(1)} %get-tuple-element.54.other, s32[8,512]{1,0:T(8,128)S(1)} %bitcast.28), custom_call_target="tpu_custom_call" | custom-call | flops 1073741824 | bytes 4194304 | tf_op jit(solution)/shard_map/layer_gather_1/pallas_call | solution.py:107
  75.7 2.8 %layer_sum_1.1.sum_own = bf16[256,512]{1,0:T(8,128)(2,1)S(1)} custom-call(s32[4]{0:T(128)S(1)} %pad_add_fusion.meta, bf16[8,256,512]{2,1,0:T(8,128)(2,1)S(1)} %layer_gather_1.1.gathered, f32[256,512]{1,0:T(8,128)S(1)} %get-tuple-element.55.recv, bf16[64,512]{1,0:T(8,128)(2,1)S(1)} %collective-permute-done.12.near, ...), custom_call_target="tpu_custom_call" | custom-call | flops 268435456 | bytes 524288 | tf_op jit(solution)/shard_map/layer_sum_1/pallas_call | solution.py:107
  80.1 2.2 %last_update.1 = (bf16[512,256]{1,0:T(8,128)(2,1)}, bf16[512,512]{1,0:T(8,128)(2,1)S(1)}) custom-call(s32[4]{0:T(128)S(1)} %pad_add_fusion.meta, bf16[256,512]{1,0:T(8,128)(2,1)S(1)} %get-tuple-element.50.own.now_own, bf16[256,512]{1,0:T(8,128)(2,1)S(1)} %collective-permute-done.11.other.now_other, f32[256,512]{1,0:T(8,128)S(1)} %get-tuple-element.51.self_own, ...), custom_call_target="tpu_custom_call" | custom-call | flops 536870912 | bytes 1572864 | tf_op jit(solution)/shard_map/last_update/pallas_call | solution.py:107
  82.7 4.4 %decode_prepare.1 = (bf16[512,512]{1,0:T(8,128)(2,1)S(1)}, bf16[1024,512]{1,0:T(8,128)(2,1)S(1)}, bf16[1024,512]{1,0:T(8,128)(2,1)S(1)}, f32[1024,256]{1,0:T(8,128)S(1)}) custom-call(s32[4]{0:T(128)S(1)} %pad_add_fusion.meta, bf16[1024,256]{1,0:T(8,128)(2,1)S(1)} %copy-done.3, bf16[1024,256]{1,0:T(8,128)(2,1)S(1)} %collective-permute-done.other, ...), custom_call_target="tpu_custom_call" | custom-call | flops 3221225472 | bytes 7340032 | tf_op jit(solution)/shard_map/decode_prepare/pallas_call | solution.py:107
  87.1 1.8 %decode_own.1.refs_0_ = f32[1024,512]{1,0:T(8,128)S(1)} custom-call(s32[4]{0:T(128)S(1)} %pad_add_fusion.meta, bf16[512,512]{1,0:T(8,128)(2,1)S(1)} %get-tuple-element.60.sent, bf16[512,512]{1,0:T(8,128)(2,1)S(1)} %get-tuple-element.63.before, s32[5,1024]{1,0:T(8,128)S(1)} %get-tuple-element.67.senders, s32[5,1024]{1,0:T(8,128)S(1)} %bitcast.23, ...), custom_call_target="tpu_custom_call" | custom-call | flops 805306368 | bytes 4194304 | tf_op jit(solution)/shard_map/decode_own/pallas_call | solution.py:107
  88.9 5.7 %collective-permute-done.17.sent = bf16[512,512]{1,0:T(8,128)(2,1)S(1)} collective-permute-done((bf16[512,512]{1,0:T(8,128)(2,1)S(1)}, bf16[512,512]{1,0:T(8,128)(2,1)S(1)}, u32[]{:S(2)}, u32[]{:S(2)}) %collective-permute-start.17) | collective-permute-done | bytes 524320 | tf_op jit(solution)/shard_map/ppermute | solution.py:56
  94.6 2.8 %decode_line.1.refs_0_ = f32[1024,512]{1,0:T(8,128)S(1)} custom-call(s32[4]{0:T(128)S(1)} %pad_add_fusion.meta, bf16[512,512]{1,0:T(8,128)(2,1)S(1)} %collective-permute-done.17.sent, bf16[1024,512]{1,0:T(8,128)(2,1)S(1)} %get-tuple-element.62.before, s32[5,1024]{1,0:T(8,128)S(1)} %get-tuple-element.67.senders, s32[5,1024]{1,0:T(8,128)S(1)} %bitcast.24, ...), custom_call_target="tpu_custom_call" | custom-call | flops 1610612736 | bytes 4194304 | tf_op jit(solution)/shard_map/decode_line/pallas_call | solution.py:107
  97.4 5.5 %collective-permute-done.16.sent = bf16[512,512]{1,0:T(8,128)(2,1)S(1)} collective-permute-done((bf16[512,512]{1,0:T(8,128)(2,1)S(1)}, bf16[512,512]{1,0:T(8,128)(2,1)S(1)}, u32[]{:S(2)}, u32[]{:S(2)}) %collective-permute-start.16) | collective-permute-done | bytes 524320 | tf_op jit(solution)/shard_map/ppermute | solution.py:56
  102.9 2.8 %decode_far.1.sum_own = bf16[1024,512]{1,0:T(8,128)(2,1)S(1)} custom-call(s32[4]{0:T(128)S(1)} %pad_add_fusion.meta, bf16[512,512]{1,0:T(8,128)(2,1)S(1)} %collective-permute-done.16.sent, bf16[1024,512]{1,0:T(8,128)(2,1)S(1)} %get-tuple-element.61.before, s32[5,1024]{1,0:T(8,128)S(1)} %get-tuple-element.67.senders, s32[5,1024]{1,0:T(8,128)S(1)} %bitcast.25, ...), custom_call_target="tpu_custom_call" | custom-call | flops 1610612736 | bytes 2097152 | tf_op jit(solution)/shard_map/decode_far/pallas_call | solution.py:107
  105.8 2.6 %collective-permute-done.18.sum_other = bf16[1024,512]{1,0:T(8,128)(2,1)S(1)} collective-permute-done((bf16[1024,512]{1,0:T(8,128)(2,1)S(1)}, bf16[1024,512]{1,0:T(8,128)(2,1)S(1)}, u32[]{:S(2)}, u32[]{:S(2)}) %collective-permute-start.18) | collective-permute-done | bytes 1048608 | tf_op jit(solution)/shard_map/ppermute | solution.py:22
  108.4 1.9 %final_update.1 = bf16[1024,256]{1,0:T(8,128)(2,1)} custom-call(s32[4]{0:T(128)S(1)} %pad_add_fusion.meta, bf16[1024,256]{1,0:T(8,128)(2,1)S(1)} %copy-done.3, f32[1024,256]{1,0:T(8,128)S(1)} %get-tuple-element.59.self_term, bf16[1024,512]{1,0:T(8,128)(2,1)S(1)} %decode_far.1.sum_own, bf16[1024,512]{1,0:T(8,128)(2,1)S(1)} %collective-permute-done.18.sum_other, ...), custom_call_target="tpu_custom_call" | custom-call | flops 268435456 | bytes 1048576 | tf_op jit(solution)/shard_map/final_update/pallas_call | solution.py:107
  (63 shorter events, 18.2 us)
Async XLA Ops:
  0.6 7.6 %collective-permute-start = (bf16[1024,256]{1,0:T(8,128)(2,1)}, bf16[1024,256]{1,0:T(8,128)(2,1)S(1)}, u32[]{:S(2)}, u32[]{:S(2)}) collective-permute-start(bf16[1024,256]{1,0:T(8,128)(2,1)} %own.11), channel_id=1, source_target_pairs={{0,1},{1,0},{2,3},{3,2},{4,5},{5,4},{6,7},{7,6},{8,9},{9,8},{10,11... | collective-permute-start | bytes 1572872 | tf_op jit(solution)/shard_map/ppermute | solution.py:22
  4.9 3.2 %collective-permute-start.1 = (bf16[512,256]{1,0:T(8,128)(2,1)S(1)}, bf16[512,256]{1,0:T(8,128)(2,1)S(1)}, u32[]{:S(2)}, u32[]{:S(2)}) collective-permute-start(bf16[512,256]{1,0:T(8,128)(2,1)S(1)} %slice_bitcast_fusion), channel_id=1, source_target_pairs={{0,1},{1,0},{2,3},{3,2},{4,5},{5,4},{6,7},{7,6},{8,9},{9,8},{10,11... | collective-permute-start | bytes 786440 | tf_op jit(solution)/shard_map/ppermute | solution.py:22
  8.2 5.9 %copy-start.4 = (bf16[512,256]{1,0:T(8,128)(2,1)S(1)}, bf16[512,256]{1,0:T(8,128)(2,1)}, u32[]{:S(2)}) copy-start(bf16[512,256]{1,0:T(8,128)(2,1)} %own.9) | copy-start | bytes 786436
  8.2 14.6 %copy-start.10 = (s32[1,5,512]{2,0,1:T(1,128)S(1)}, s32[1,5,512]{2,0,1:T(1,128)}, u32[]{:S(2)}) copy-start(s32[1,5,512]{2,0,1:T(1,128)} %param.20) | copy-start | bytes 30724
  8.2 14.6 %copy-start.11 = (s32[1,5,512]{2,0,1:T(1,128)S(1)}, s32[1,5,512]{2,0,1:T(1,128)}, u32[]{:S(2)}) copy-start(s32[1,5,512]{2,0,1:T(1,128)} %param.19) | copy-start | bytes 30724
  10.7 32.6 %collective-permute-start.7 = (bf16[2,4,512,256]{3,2,1,0:T(8,128)(2,1)S(1)}, bf16[2,4,512,256]{3,2,1,0:T(8,128)(2,1)S(1)}, u32[]{:S(2)}, u32[]{:S(2)}) collective-permute-start(bf16[2,4,512,256]{3,2,1,0:T(8,128)(2,1)S(1)} %copy-done), channel_id=1, source_target_pairs={{0,1},{1,0},{2,3},{3,2},{4,5},{5,4},{6,7},{7,6},{8,9},{9,8},{10,11... | collective-permute-start | bytes 6291464 | tf_op jit(solution)/shard_map/ppermute | solution.py:22
  11.3 12.7 %collective-permute-start.3 = (bf16[4,512,256]{2,1,0:T(8,128)(2,1)}, bf16[4,512,256]{2,1,0:T(8,128)(2,1)S(1)}, u32[]{:S(2)}, u32[]{:S(2)}) collective-permute-start(bf16[4,512,256]{2,1,0:T(8,128)(2,1)} %w3.4), channel_id=1, source_target_pairs={{0,1},{1,0},{2,3},{3,2},{4,5},{5,4},{6,7},{7,6},{8,9},{9,8},{10,11... | collective-permute-start | bytes 3145736 | tf_op jit(solution)/shard_map/ppermute | solution.py:22
  12.7 18.0 %collective-permute-start.5 = (bf16[512,512]{1,0:T(8,128)(2,1)S(1)}, bf16[512,512]{1,0:T(8,128)(2,1)S(1)}, u32[]{:S(2)}, u32[]{:S(2)}) collective-permute-start(bf16[512,512]{1,0:T(8,128)(2,1)S(1)} %encode_line.1), channel_id=1, source_target_pairs={{0,2},{1,5},{2,0},{3,7},{4,6},{5,1},{6,4},{7,3},{8,10},{9,13},{10,... | collective-permute-start | bytes 1572872 | tf_op jit(solution)/shard_map/ppermute | solution.py:56
  13.8 26.7 %collective-permute-start.4 = (bf16[512,512]{1,0:T(8,128)(2,1)S(1)}, bf16[512,512]{1,0:T(8,128)(2,1)S(1)}, u32[]{:S(2)}, u32[]{:S(2)}) collective-permute-start(bf16[512,512]{1,0:T(8,128)(2,1)S(1)} %get-tuple-element.37), channel_id=1, source_target_pairs={{0,254},{1,3},{2,4},{3,1},{4,2},{5,9},{6,8},{7,11},{8,6},{9,5},{10... | collective-permute-start | bytes 1572872 | tf_op jit(solution)/shard_map/ppermute | solution.py:56
  14.1 9.8 %collective-permute-start.2 = (bf16[512,256]{1,0:T(8,128)(2,1)S(1)}, bf16[512,256]{1,0:T(8,128)(2,1)S(1)}, u32[]{:S(2)}, u32[]{:S(2)}) collective-permute-start(bf16[512,256]{1,0:T(8,128)(2,1)S(1)} %copy-done.4), channel_id=1, source_target_pairs={{0,1},{1,0},{2,3},{3,2},{4,5},{5,4},{6,7},{7,6},{8,9},{9,8},{10,11... | collective-permute-start | bytes 786440 | tf_op jit(solution)/shard_map/ppermute | solution.py:22
  41.7 1.6 %collective-permute-start.6 = (bf16[256,512]{1,0:T(8,128)(2,1)S(1)}, bf16[256,512]{1,0:T(8,128)(2,1)S(1)}, u32[]{:S(2)}, u32[]{:S(2)}) collective-permute-start(bf16[256,512]{1,0:T(8,128)(2,1)S(1)} %get-tuple-element.42), channel_id=1, source_target_pairs={{0,1},{1,0},{2,3},{3,2},{4,5},{5,4},{6,7},{7,6},{8,9},{9,8},{10,11... | collective-permute-start | bytes 786440 | tf_op jit(solution)/shard_map/ppermute | solution.py:22
  45.0 11.3 %collective-permute-start.8 = (bf16[256,512]{1,0:T(8,128)(2,1)S(1)}, bf16[256,512]{1,0:T(8,128)(2,1)S(1)}, u32[]{:S(2)}, u32[]{:S(2)}) collective-permute-start(bf16[256,512]{1,0:T(8,128)(2,1)S(1)} %get-tuple-element.44.own.now), channel_id=1, source_target_pairs={{0,1},{1,0},{2,3},{3,2},{4,5},{5,4},{6,7},{7,6},{8,9},{9,8},{10,11... | collective-permute-start | bytes 786440 | tf_op jit(solution)/shard_map/ppermute | solution.py:22
  45.2 33.4 %collective-permute-start.15 = (bf16[4,512,256]{2,1,0:T(8,128)(2,1)S(1)}, bf16[4,512,256]{2,1,0:T(8,128)(2,1)S(1)}, u32[]{:S(2)}, u32[]{:S(2)}) collective-permute-start(bf16[4,512,256]{2,1,0:T(8,128)(2,1)S(1)} %copy-done.1), channel_id=1, source_target_pairs={{0,1},{1,0},{2,3},{3,2},{4,5},{5,4},{6,7},{7,6},{8,9},{9,8},{10,11... | collective-permute-start | bytes 3145736 | tf_op jit(solution)/shard_map/ppermute | solution.py:22
  45.6 12.0 %copy-start.5 = (s32[512,8]{0,1:T(8,128)S(1)}, s32[512,8]{0,1:T(8,128)}, u32[]{:S(2)}) copy-start(s32[512,8]{0,1:T(8,128)} %param.21) | copy-start | bytes 49156
  45.6 3.7 %collective-permute-start.9 = (bf16[64,512]{1,0:T(8,128)(2,1)S(1)}, bf16[64,512]{1,0:T(8,128)(2,1)S(1)}, u32[]{:S(2)}, u32[]{:S(2)}) collective-permute-start(bf16[64,512]{1,0:T(8,128)(2,1)S(1)} %get-tuple-element.48), channel_id=1, source_target_pairs={{1,2},{2,1},{3,4},{4,3},{5,6},{6,5},{7,8},{8,7},{9,10},{10,9},{11,... | collective-permute-start | bytes 196616 | tf_op jit(solution)/shard_map/ppermute | solution.py:56
  49.3 10.2 %collective-permute-start.10 = (bf16[64,512]{1,0:T(8,128)(2,1)S(1)}, bf16[64,512]{1,0:T(8,128)(2,1)S(1)}, u32[]{:S(2)}, u32[]{:S(2)}) collective-permute-start(bf16[64,512]{1,0:T(8,128)(2,1)S(1)} %collective-permute-done.9.near), channel_id=1, source_target_pairs={{0,1},{1,0},{2,3},{3,2},{4,5},{5,4},{6,7},{7,6},{8,9},{9,8},{10,11... | collective-permute-start | bytes 196616 | tf_op jit(solution)/shard_map/ppermute | solution.py:22
  62.7 9.7 %collective-permute-start.11 = (bf16[256,512]{1,0:T(8,128)(2,1)S(1)}, bf16[256,512]{1,0:T(8,128)(2,1)S(1)}, u32[]{:S(2)}, u32[]{:S(2)}) collective-permute-start(bf16[256,512]{1,0:T(8,128)(2,1)S(1)} %get-tuple-element.50.own.now_own), channel_id=1, source_target_pairs={{0,1},{1,0},{2,3},{3,2},{4,5},{5,4},{6,7},{7,6},{8,9},{9,8},{10,11... | collective-permute-start | bytes 786440 | tf_op jit(solution)/shard_map/ppermute | solution.py:22
  62.8 3.8 %collective-permute-start.12 = (bf16[64,512]{1,0:T(8,128)(2,1)S(1)}, bf16[64,512]{1,0:T(8,128)(2,1)S(1)}, u32[]{:S(2)}, u32[]{:S(2)}) collective-permute-start(bf16[64,512]{1,0:T(8,128)(2,1)S(1)} %get-tuple-element.56), channel_id=1, source_target_pairs={{1,2},{2,1},{3,4},{4,3},{5,6},{6,5},{7,8},{8,7},{9,10},{10,9},{11,... | collective-permute-start | bytes 196616 | tf_op jit(solution)/shard_map/ppermute | solution.py:56
  66.6 9.1 %collective-permute-start.13 = (bf16[64,512]{1,0:T(8,128)(2,1)S(1)}, bf16[64,512]{1,0:T(8,128)(2,1)S(1)}, u32[]{:S(2)}, u32[]{:S(2)}) collective-permute-start(bf16[64,512]{1,0:T(8,128)(2,1)S(1)} %collective-permute-done.12.near), channel_id=1, source_target_pairs={{0,1},{1,0},{2,3},{3,2},{4,5},{5,4},{6,7},{7,6},{8,9},{9,8},{10,11... | collective-permute-start | bytes 196616 | tf_op jit(solution)/shard_map/ppermute | solution.py:22
  75.7 2.9 %copy-start.7 = (s32[1,5,1024]{2,0,1:T(1,128)S(1)}, s32[1,5,1024]{2,0,1:T(1,128)}, u32[]{:S(2)}) copy-start(s32[1,5,1024]{2,0,1:T(1,128)} %param.24) | copy-start | bytes 61444
  78.5 1.6 %collective-permute-start.14 = (bf16[256,512]{1,0:T(8,128)(2,1)S(1)}, bf16[256,512]{1,0:T(8,128)(2,1)S(1)}, u32[]{:S(2)}, u32[]{:S(2)}) collective-permute-start(bf16[256,512]{1,0:T(8,128)(2,1)S(1)} %layer_sum_1.1.sum_own), channel_id=1, source_target_pairs={{0,1},{1,0},{2,3},{3,2},{4,5},{5,4},{6,7},{7,6},{8,9},{9,8},{10,11... | collective-permute-start | bytes 786440 | tf_op jit(solution)/shard_map/ppermute | solution.py:22
  82.3 12.2 %collective-permute-start.17 = (bf16[512,512]{1,0:T(8,128)(2,1)S(1)}, bf16[512,512]{1,0:T(8,128)(2,1)S(1)}, u32[]{:S(2)}, u32[]{:S(2)}) collective-permute-start(bf16[512,512]{1,0:T(8,128)(2,1)S(1)} %get-tuple-element.60.sent), channel_id=1, source_target_pairs={{0,2},{1,5},{2,0},{3,7},{4,6},{5,1},{6,4},{7,3},{8,10},{9,13},{10,... | collective-permute-start | bytes 1572872 | tf_op jit(solution)/shard_map/ppermute | solution.py:56
  82.4 20.5 %collective-permute-start.16 = (bf16[512,512]{1,0:T(8,128)(2,1)S(1)}, bf16[512,512]{1,0:T(8,128)(2,1)S(1)}, u32[]{:S(2)}, u32[]{:S(2)}) collective-permute-start(bf16[512,512]{1,0:T(8,128)(2,1)S(1)} %get-tuple-element.60.sent), channel_id=1, source_target_pairs={{0,254},{1,3},{2,4},{3,1},{4,2},{5,9},{6,8},{7,11},{8,6},{9,5},{10... | collective-permute-start | bytes 1572872 | tf_op jit(solution)/shard_map/ppermute | solution.py:56
  105.7 2.7 %collective-permute-start.18 = (bf16[1024,512]{1,0:T(8,128)(2,1)S(1)}, bf16[1024,512]{1,0:T(8,128)(2,1)S(1)}, u32[]{:S(2)}, u32[]{:S(2)}) collective-permute-start(bf16[1024,512]{1,0:T(8,128)(2,1)S(1)} %decode_far.1.sum_own), channel_id=1, source_target_pairs={{0,1},{1,0},{2,3},{3,2},{4,5},{5,4},{6,7},{7,6},{8,9},{9,8},{10,11... | collective-permute-start | bytes 3145736 | tf_op jit(solution)/shard_map/ppermute | solution.py:22
  (7 other events, 14.4 us)
